TPU v7x, 256 devices: a whole 4x4x8 slice. The times are simulated.
256 devices in a mesh: rep: 8 (over y_hi, x), ep: 32 (over z, y_lo, core).
Axes of the slice: x: 4, y: 4 (y_hi: 2, y_lo: 2; y = y_hi * 2 + y_lo), z: 8, core: 2. Of those that a mesh axis runs over, the one named last changes fastest.
Arguments:
- tokens: bfloat16 [32768, 1024], P(('rep', 'ep')), may hold values from -6 to 6
- expert_ids: int32 [32768, 4], P(('rep', 'ep')), may hold values from 0 to 31, all different within a row; in each aligned block of 128 rows (0 to 127, 128 to 255, ...) at most 32 rows name the same one
- gate_probs: float32 [32768, 4], P(('rep', 'ep')), may hold values from 0.05 to 1
- out_grad: bfloat16 [32768, 1024], P(('rep', 'ep')), may hold values from -0.75 to 0.75
- w_in: bfloat16 [32, 1024, 1024], P('ep'), may hold values from -0.1875 to 0.1875
- w_out: bfloat16 [32, 1024, 1024], P('ep'), may hold values from -0.1875 to 0.1875
Outputs:
- mixed: bfloat16 [32768, 1024], P(('rep', 'ep'))
- token_grad: bfloat16 [32768, 1024], P(('rep', 'ep'))
- gate_grad: float32 [32768, 4], P(('rep', 'ep'))
- in_weight_grad: float32 [32, 1024, 1024], P('ep', 'rep')
- out_weight_grad: float32 [32, 1024, 1024], P('ep', 'rep')
Inputs may be any that keep to these rules, and one draw needn't show every extreme that they name: `expert_ids`: each token names 4 different experts. Within each device's block of 128 tokens no expert is named by more than 32 tokens, and in every draw some expert is named by exactly 32 tokens of some block.
All inputs are finite; a program needn't handle non-finite values.
Results may differ from a plain program's by a relative error of at most 0.014.
Values may be sent and summed in bfloat16 or wider, within the bound.
A program may use at most 64 MiB of HBM per device.

v0:
```python
import jax
import jax.numpy as jnp
from jax import lax
from jax.sharding import PartitionSpec as P

ROOT_HALF = 0.7071067811865476
INV_ROOT_TAU = 0.3989422804014327


def gelu_value(preact):
    return 0.5 * preact * (1.0 + lax.erf(preact * ROOT_HALF))


def gelu_slope(preact):
    return 0.5 * (1.0 + lax.erf(preact * ROOT_HALF)) + preact * INV_ROOT_TAU * jnp.exp(
        -0.5 * preact * preact
    )


def expert_forward(arrived, w_in, w_out):
    preact = jnp.einsum("slcd,ldh->slch", arrived, w_in, preferred_element_type=jnp.float32)
    activated = gelu_value(preact).astype(jnp.bfloat16)
    expert_out = jnp.einsum(
        "slch,lhd->slcd", activated, w_out, preferred_element_type=jnp.float32
    ).astype(jnp.bfloat16)
    return (preact, activated, expert_out)


def expert_backward(preact, out_rows, w_in, w_out):
    act_grad = jnp.einsum("slcd,lhd->slch", out_rows, w_out, preferred_element_type=jnp.float32)
    pre_grad = (act_grad * gelu_slope(preact)).astype(jnp.bfloat16)
    row_grads = jnp.einsum(
        "slch,ldh->slcd", pre_grad, w_in, preferred_element_type=jnp.float32
    ).astype(jnp.bfloat16)
    return (pre_grad, row_grads)


def body(tokens, expert_ids, gate_probs, out_grad, w_in, w_out):
    tok_rows, features = tokens.shape
    top_count = expert_ids.shape[1]
    local_count = w_in.shape[0]
    sources = lax.axis_size("ep")
    experts = local_count * sources
    capacity = 2 * tok_rows * top_count // experts
    flat_ids = expert_ids.reshape(-1)
    onehot = (flat_ids[:, None] == jnp.arange(experts, dtype=jnp.int32)[None, :]).astype(jnp.int32)
    earlier = jnp.cumsum(onehot, axis=0) - onehot
    target = flat_ids * capacity + jnp.sum(earlier * onehot, axis=1)

    def place_rows(rows):
        filled = jnp.zeros((experts * capacity, features), rows.dtype).at[target].set(rows)
        return filled.reshape(sources, local_count * capacity, features)

    def open_rows(sent):
        return sent.reshape(sources, local_count, capacity, features)

    def close_rows(result):
        return result.reshape(sources, local_count * capacity, features)

    x_sent = place_rows(jnp.repeat(tokens, top_count, axis=0))
    g_rows = (
        gate_probs.reshape(-1)[:, None]
        * jnp.repeat(out_grad, top_count, axis=0).astype(jnp.float32)
    ).astype(jnp.bfloat16)
    g_sent = place_rows(g_rows)
    arrived = open_rows(lax.all_to_all(x_sent, "ep", split_axis=0, concat_axis=0, tiled=True))
    preact, activated, expert_out = expert_forward(arrived, w_in, w_out)
    out_back = lax.all_to_all(close_rows(expert_out), "ep", split_axis=0, concat_axis=0, tiled=True)
    out_rows = open_rows(lax.all_to_all(g_sent, "ep", split_axis=0, concat_axis=0, tiled=True))
    pre_grad, row_grads = expert_backward(preact, out_rows, w_in, w_out)
    grad_back = lax.all_to_all(close_rows(row_grads), "ep", split_axis=0, concat_axis=0, tiled=True)
    part = arrived
    grad_in = lax.psum_scatter(
        jnp.einsum("slcd,slch->dlh", part, pre_grad, preferred_element_type=jnp.float32).astype(
            jnp.bfloat16
        ),
        "rep",
        scatter_dimension=0,
        tiled=True,
    ).astype(jnp.float32)
    part = activated
    grad_out = lax.psum_scatter(
        jnp.einsum("slch,slcd->hld", part, out_rows, preferred_element_type=jnp.float32).astype(
            jnp.bfloat16
        ),
        "rep",
        scatter_dimension=0,
        tiled=True,
    ).astype(jnp.float32)
    picked = out_back.reshape(experts * capacity, features)[target]
    picked = picked.reshape(tok_rows, top_count, features).astype(jnp.float32)
    mixed = jnp.sum(gate_probs[:, :, None] * picked, axis=1).astype(jnp.bfloat16)
    gate_grad = jnp.sum(out_grad.astype(jnp.float32)[:, None, :] * picked, axis=2)
    picked_grad = grad_back.reshape(experts * capacity, features)[target]
    picked_grad = picked_grad.reshape(tok_rows, top_count, features).astype(jnp.float32)
    token_grad = jnp.sum(picked_grad, axis=1).astype(jnp.bfloat16)
    return (mixed, token_grad, gate_grad, jnp.moveaxis(grad_in, 1, 0), jnp.moveaxis(grad_out, 1, 0))


def solution(mesh):
    placed = (
        P(("rep", "ep"), None),
        P(("rep", "ep"), None),
        P(("rep", "ep"), None),
        P(("rep", "ep"), None),
        P("ep", None, None),
        P("ep", None, None),
    )
    return jax.shard_map(
        body,
        mesh=mesh,
        in_specs=placed,
        out_specs=(
            P(("rep", "ep"), None),
            P(("rep", "ep"), None),
            P(("rep", "ep"), None),
            P("ep", "rep", None),
            P("ep", "rep", None),
        ),
        check_vma=False,
    )
```

profile of v0, /device:TPU:1, one launch (start us, length us, event | category | flops | bytes accessed | tf_op | source)
XLA Modules:
  0.0 348.3 jit_solution(13910959107386548663)
XLA Ops:
  9.0 1.2 reduce-window.6
  10.7 1.3 broadcast_in_dim.4
  12.0 1.1 reshape.164
  13.2 4.8 %scatter_custom_fusion = bf16[1024,1024]{1,0:T(8,128)(2,1)} fusion(s32[512]{0:T(512)S(1)} %bitcast.125, bf16[512,1024]{1,0:T(8,128)(2,1)} %reshape.164, bf16[]{:T(256)} %constant.10.clone.1), kind=kCustom, calls=%fused_computation.39 | custom fusion | bytes 2097664 | tf_op jit(solution)/shard_map/scatter | solution.py:51
  18.0 11.3 %all-to-all-start = ((bf16[32,32,1024]{2,1,0:T(8,128)(2,1)}), bf16[32,32,1024]{2,1,0:T(8,128)(2,1)}, u32[]{:S(2)}, u32[]{:S(2)}) async-start(bf16[32,32,1024]{2,1,0:T(8,128)(2,1)} %bitcast.123), calls=%async_computation | async-start | bytes 4194304 | tf_op jit(solution)/shard_map/all_to_all | solution.py:66
  29.6 1.9 broadcast_in_dim.5
  31.5 2.9 convert_element_type.79
  34.4 5.3 %scatter_custom_fusion.1 = bf16[1024,1024]{1,0:T(8,128)(2,1)} fusion(s32[512]{0:T(512)S(1)} %bitcast.126, f32[512,1024]{1,0:T(8,128)} %convert_element_type.79, f32[512]{0:T(512)S(1)} %mul.90, bf16[]{:T(256)} %constant.10.clone.1), kind=kCustom, calls=%fused_computation.36 | custom fusion | flops 1048576 | bytes 4196354 | tf_op jit(solution)/shard_map/scatter | solution.py:51
  39.7 39.7 %all-to-all-done = bf16[32,32,1024]{2,1,0:T(8,128)(2,1)} async-done(((bf16[32,32,1024]{2,1,0:T(8,128)(2,1)}), bf16[32,32,1024]{2,1,0:T(8,128)(2,1)}, u32[]{:S(2)}, u32[]{:S(2)}) %all-to-all-start) | async-done | bytes 2097184 | tf_op jit(solution)/shard_map/all_to_all | solution.py:66
  79.5 4.9 %all-to-all-start.2 = ((bf16[32,32,1024]{2,1,0:T(8,128)(2,1)}), bf16[32,32,1024]{2,1,0:T(8,128)(2,1)}, u32[]{:S(2)}, u32[]{:S(2)}) async-start(bf16[32,32,1024]{2,1,0:T(8,128)(2,1)} %bitcast.124), calls=%async_computation.2 | async-start | bytes 4194304 | tf_op jit(solution)/shard_map/all_to_all | solution.py:69
  84.4 5.8 %fusion.17 = f32[32,32,1024]{2,1,0:T(8,128)} fusion(bf16[32,32,1024]{2,1,0:T(8,128)(2,1)} %all-to-all-done, bf16[1,1024,1024]{2,1,0:T(8,128)(2,1)S(1)} %copy-done), kind=kOutput, calls=%fused_computation.27 | convolution fusion | flops 2147483648 | bytes 8388608 | tf_op jit(solution)/shard_map/slcd,ldh->slch/dot_general | solution.py:21
  90.3 44.1 %all-to-all-done.2 = bf16[32,32,1024]{2,1,0:T(8,128)(2,1)} async-done(((bf16[32,32,1024]{2,1,0:T(8,128)(2,1)}), bf16[32,32,1024]{2,1,0:T(8,128)(2,1)}, u32[]{:S(2)}, u32[]{:S(2)}) %all-to-all-start.2) | async-done | bytes 2097184 | tf_op jit(solution)/shard_map/all_to_all | solution.py:69
  134.4 6.2 %fusion.4 = bf16[32,1,32,1024]{3,2,0,1:T(8,128)(2,1)S(1)} fusion(f32[32,32,1024]{2,1,0:T(8,128)} %fusion.17, bf16[32,32,1024]{2,1,0:T(8,128)(2,1)} %all-to-all-done.2, bf16[1,1024,1024]{2,1,0:T(8,128)(2,1)} %param.11), kind=kOutput, calls=%fused_computation.9 | convolution fusion | flops 2157969408 | bytes 10485760 | tf_op jit(solution)/shard_map/slcd,lhd->slch/dot_general | solution.py:30
  140.6 1.3 copy-done.3
  141.9 3.8 %fusion.22 = bf16[32,32,1024]{2,1,0:T(8,128)(2,1)} fusion(bf16[1,1024,1024]{2,1,0:T(8,128)(2,1)S(1)} %copy-done, bf16[32,1,32,1024]{3,2,0,1:T(8,128)(2,1)S(1)} %fusion.4), kind=kOutput, calls=%fused_computation.33 | convolution fusion | flops 2148532224 | bytes 6291456 | tf_op jit(solution)/shard_map/slch,ldh->slcd/dot_general | solution.py:32
  145.7 5.1 %all-to-all-start.3 = ((bf16[32,32,1024]{2,1,0:T(8,128)(2,1)}), bf16[32,32,1024]{2,1,0:T(8,128)(2,1)}, u32[]{:S(2)}, u32[]{:S(2)}) async-start(bf16[32,32,1024]{2,1,0:T(8,128)(2,1)} %fusion.22), calls=%async_computation.3 | async-start | bytes 4194304 | tf_op jit(solution)/shard_map/all_to_all | solution.py:71
  150.8 5.9 %fusion.27 = bf16[1024,1024]{0,1:T(8,128)(2,1)} fusion(bf16[32,32,1024]{2,1,0:T(8,128)(2,1)} %all-to-all-done, bf16[32,1,32,1024]{3,2,0,1:T(8,128)(2,1)} %copy-done.3), kind=kOutput, calls=%fused_computation.34 | convolution fusion | flops 2148532224 | bytes 6291456 | tf_op jit(solution)/shard_map/slcd,slch->dlh/dot_general | solution.py:74
  156.7 3.9 %copy.43 = bf16[1024,1024]{1,0:T(8,128)(2,1)} copy(bf16[1024,1024]{0,1:T(8,128)(2,1)} %fusion.27) | data formatting | bytes 4194304
  160.7 6.5 %fusion.19 = bf16[32,32,1024]{2,1,0:T(8,128)(2,1)} fusion(bf16[1,1024,1024]{2,1,0:T(8,128)(2,1)} %param.11, f32[32,32,1024]{2,1,0:T(8,128)} %fusion.17), kind=kOutput, calls=%fused_computation.32 | convolution fusion | flops 2153775104 | bytes 8388608 | tf_op jit(solution)/shard_map/slch,lhd->slcd/dot_general | solution.py:23
  167.2 33.7 %all-to-all-done.3 = bf16[32,32,1024]{2,1,0:T(8,128)(2,1)} async-done(((bf16[32,32,1024]{2,1,0:T(8,128)(2,1)}), bf16[32,32,1024]{2,1,0:T(8,128)(2,1)}, u32[]{:S(2)}, u32[]{:S(2)}) %all-to-all-start.3) | async-done | bytes 2097184 | tf_op jit(solution)/shard_map/all_to_all | solution.py:71
  200.9 4.9 %all-to-all-start.1 = ((bf16[32,32,1024]{2,1,0:T(8,128)(2,1)}), bf16[32,32,1024]{2,1,0:T(8,128)(2,1)}, u32[]{:S(2)}, u32[]{:S(2)}) async-start(bf16[32,32,1024]{2,1,0:T(8,128)(2,1)} %fusion.19), calls=%async_computation.1 | async-start | bytes 4194304 | tf_op jit(solution)/shard_map/all_to_all | solution.py:68
  206.1 6.7 %fusion.30 = bf16[1024,1024]{0,1:T(8,128)(2,1)} fusion(bf16[32,32,1024]{2,1,0:T(8,128)(2,1)} %all-to-all-done.2, f32[32,32,1024]{2,1,0:T(8,128)} %fusion.17), kind=kOutput, calls=%fused_computation.35 | convolution fusion | flops 2153775104 | bytes 8388608 | tf_op jit(solution)/shard_map/slch,slcd->hld/dot_general | solution.py:83
  212.7 4.0 %copy.45 = bf16[1024,1024]{1,0:T(8,128)(2,1)} copy(bf16[1024,1024]{0,1:T(8,128)(2,1)} %fusion.30) | data formatting | bytes 4194304
  217.5 4.6 %gather_fusion.1 = bf16[512,1024]{1,0:T(8,128)(2,1)S(1)} fusion(bf16[1024,1024]{1,0:T(8,128)(2,1)} %bitcast.20, s32[1024]{0:T(1024)S(1)} %pad_clamp_fusion), kind=kCustom, calls=%fused_computation.1 | custom fusion | bytes 2099200 | tf_op jit(solution)/shard_map/gather | solution.py:94
  222.1 1.3 reshape.140
  223.4 3.2 reduce_sum.44
  226.6 29.2 %all-to-all-done.1 = bf16[32,32,1024]{2,1,0:T(8,128)(2,1)} async-done(((bf16[32,32,1024]{2,1,0:T(8,128)(2,1)}), bf16[32,32,1024]{2,1,0:T(8,128)(2,1)}, u32[]{:S(2)}, u32[]{:S(2)}) %all-to-all-start.1) | async-done | bytes 2097184 | tf_op jit(solution)/shard_map/all_to_all | solution.py:68
  255.9 4.6 %gather_fusion = bf16[512,1024]{1,0:T(8,128)(2,1)S(1)} fusion(bf16[1024,1024]{1,0:T(8,128)(2,1)} %bitcast.14, s32[1024]{0:T(1024)S(1)} %pad_clamp_fusion), kind=kCustom, calls=%fused_computation | custom fusion | bytes 2099200 | tf_op jit(solution)/shard_map/gather | solution.py:90
  260.5 1.7 reshape.141
  262.2 4.2 %multiply_reduce_fusion = (f32[128,4]{1,0:T(8,128)S(1)}, bf16[128,1024]{1,0:T(8,128)(2,1)}) fusion(f32[128,4,1024]{2,1,0:T(4,128)} %reshape.141, f32[128,1024]{1,0:T(8,128)} %convert_element_type.78, f32[128,4]{1,0:T(8,128)S(1)} %copy.30), kind=kLoop, calls=%fused_computation.29 | loop fusion | flops 1965568 | bytes 2887680 | tf_op jit(solution)/shard_map/reduce_sum | solution.py:93
  267.1 1.1 copy.44
  269.3 70.1 %reduce-scatter.9.cloned.1.call-done = bf16[128,1024]{1,0:T(8,128)(2,1)} async-done(((bf16[1024,1024]{1,0:T(8,128)(2,1)}), bf16[128,1024]{1,0:T(8,128)(2,1)}) %reduce-scatter.9.cloned.1.call-update) | async-done | bytes 262160
  (34 shorter events, 7.7 us)
Async XLA Ops:
  7.2 77.3 %copy-start = (bf16[1,1024,1024]{2,1,0:T(8,128)(2,1)S(1)}, bf16[1,1024,1024]{2,1,0:T(8,128)(2,1)}, u32[]{:S(2)}) copy-start(bf16[1,1024,1024]{2,1,0:T(8,128)(2,1)} %param.10) | copy-start | bytes 6291460
  18.0 11.3 %copy-start.2 = (f32[128,4]{0,1:T(4,128)S(1)}, f32[128,4]{0,1:T(4,128)}, u32[]{:S(2)}) copy-start(f32[128,4]{0,1:T(4,128)} %param.8) | copy-start | bytes 6148
  18.0 11.6 %copy-start.1 = (bf16[128,1024]{1,0:T(8,128)(2,1)S(1)}, bf16[128,1024]{1,0:T(8,128)(2,1)}, u32[]{:S(2)}) copy-start(bf16[128,1024]{1,0:T(8,128)(2,1)} %param.9) | copy-start | bytes 786436
  18.0 61.5 %all-to-all-start = ((bf16[32,32,1024]{2,1,0:T(8,128)(2,1)}), bf16[32,32,1024]{2,1,0:T(8,128)(2,1)}, u32[]{:S(2)}, u32[]{:S(2)}) async-start(bf16[32,32,1024]{2,1,0:T(8,128)(2,1)} %bitcast.123), calls=%async_computation | async-start | bytes 4194304 | tf_op jit(solution)/shard_map/all_to_all | solution.py:66
  79.5 54.9 %all-to-all-start.2 = ((bf16[32,32,1024]{2,1,0:T(8,128)(2,1)}), bf16[32,32,1024]{2,1,0:T(8,128)(2,1)}, u32[]{:S(2)}, u32[]{:S(2)}) async-start(bf16[32,32,1024]{2,1,0:T(8,128)(2,1)} %bitcast.124), calls=%async_computation.2 | async-start | bytes 4194304 | tf_op jit(solution)/shard_map/all_to_all | solution.py:69
  140.6 1.3 copy-start.3
  145.7 55.2 %all-to-all-start.3 = ((bf16[32,32,1024]{2,1,0:T(8,128)(2,1)}), bf16[32,32,1024]{2,1,0:T(8,128)(2,1)}, u32[]{:S(2)}, u32[]{:S(2)}) async-start(bf16[32,32,1024]{2,1,0:T(8,128)(2,1)} %fusion.22), calls=%async_computation.3 | async-start | bytes 4194304 | tf_op jit(solution)/shard_map/all_to_all | solution.py:71
  150.8 116.3 %reduce-scatter.7.cloned.1.call-start = ((), (), s32[]{:S(2)}) async-start(), calls=%async_computation.6 | async-start | bytes 2359296
  200.9 55.0 %all-to-all-start.1 = ((bf16[32,32,1024]{2,1,0:T(8,128)(2,1)}), bf16[32,32,1024]{2,1,0:T(8,128)(2,1)}, u32[]{:S(2)}, u32[]{:S(2)}) async-start(bf16[32,32,1024]{2,1,0:T(8,128)(2,1)} %fusion.19), calls=%async_computation.1 | async-start | bytes 4194304 | tf_op jit(solution)/shard_map/all_to_all | solution.py:68
  205.8 133.6 %reduce-scatter.9.cloned.1.call-start = ((), (), s32[]{:S(2)}) async-start(), calls=%async_computation.7 | async-start | bytes 2359296
Sparse Core Ops, SparseCore 0:
  160.8 94.3 reduce-scatter.6
  259.8 79.4 reduce-scatter.8
where the time goes:
time: 350 us; the launch traced here: 348 us
  waiting for transfers between devices  217 us (62%)
  local copies, waits for them, and re-layouts  40.2 us (11%)
  matrix products  34.9 us (10%)
  starting transfers between devices  26.5 us (8%)
  other arithmetic  15.7 us (4%)
  between operations  14.2 us (4%)
    unnamed x4, waiting for transfers between devices  70.1 us
    all_to_all x1, waiting for transfers between devices, body(): lax.all_to_all(g_sent, 'ep', split_axis=0, concat_axis=0, tiled=True)  44.1 us
    all_to_all x1, waiting for transfers between devices, body(): lax.all_to_all(x_sent, 'ep', split_axis=0, concat_axis=0, tiled=True)  39.7 us
    all_to_all x1, waiting for transfers between devices, body(): lax.all_to_all(close_rows(row_grads), 'ep', split_axis=0, concat_axis=0,...  33.7 us
    all_to_all x1, waiting for transfers between devices, body(): lax.all_to_all(close_rows(expert_out), 'ep', split_axis=0, concat_axis=0,...  29.2 us
    unnamed x17, local copies, waits for them, and re-layouts  15.1 us
    all_to_all x1, starting transfers between devices, body(): lax.all_to_all(x_sent, 'ep', split_axis=0, concat_axis=0, tiled=True)  11.3 us
  transfers between devices with their start and end apart: 6, of which 5 were waited for; matrix products, arithmetic and copies ran while one was open for 19% of the time, Pallas kernels for 0%

commit v1 on v0

v1 whole, which is shorter than its diff:
```python
import jax
import jax.numpy as jnp
from jax import lax
from jax.experimental import pallas as pl
from jax.experimental.pallas import tpu as pltpu
from jax.sharding import PartitionSpec as P

MESH = pl.DeviceIdType.MESH
BF = jnp.bfloat16
F32 = jnp.float32
NZ, NX = 8, 4
T = 128
HALF = 64
CAP = 32
D = 1024
ROOT_HALF = 0.7071067811865476
INV_ROOT_TAU = 0.3989422804014327

ORDER = (0, 7, 1, 6, 2, 5, 3, 4)
POS = {r: p for p, r in enumerate(ORDER)}
RS_UNITS = (
    ((0, 4), (1, 3), (0, 3), (1, 2), (0, 2), (1, 1), (0, 1)),
    ((1, 4), (0, 5), (1, 5), (0, 6), (1, 6), (0, 7), (1, 7)),
)


def dot(a, b, dims=((1,), (0,))):
    return lax.dot_general(a, b, (dims, ((), ())), preferred_element_type=F32)


def kernel(
    tok, grd, meta, win, wout,
    mixed_o, tgrad_o, gg_o, gin_o, gout_o,
    ball, metall, sel, selt, gatet, gslot, wi, wo,
    disp, arr, act, slope, pre, res, ret,
    rs_send, rs_recv, gg_send, gg_recv,
    wx_send, wx_recv, wx_own, wx_chain, wy_send, wy_recv,
    loc_sem, ag_s, ag_r, meta_s, meta_r, disp_s, disp_r, ret_s, ret_r,
    rs_s, rs_r, gg_s, gg_r, wx_s, wx_r, wy_s, wy_r,
):
    rep = lax.axis_index("rep")
    ep = lax.axis_index("ep")
    x, y_hi = lax.rem(rep, 4), lax.div(rep, 4)
    c, y_lo, z = lax.rem(ep, 2), lax.rem(lax.div(ep, 2), 2), lax.div(ep, 4)
    y = y_hi * 2 + y_lo

    def dev(x_, y_, z_, c_):
        return (lax.div(y_, 2) * 4 + x_, (z_ * 2 + lax.rem(y_, 2)) * 2 + c_)

    def along_z(r):
        return dev(x, y, lax.rem(z + r, 8), c)

    y_up, y_dn = lax.rem(y + 1, 4), lax.rem(y + 3, 4)
    y_to = lax.rem(y + 1 + 2 * c, 4)
    y_from_other = lax.rem(y + 1 + 2 * c, 4)
    y_from_same = lax.rem(y + 3 - 2 * c, 4)
    other = 1 - c
    to_plane = (None, dev(x, y, z, other), dev(x, y_to, z, c), dev(x, y_to, z, other))
    from_plane = (
        None, dev(x, y, z, other), dev(x, y_from_same, z, c), dev(x, y_from_other, z, other),
    )
    x_right, x_left = dev(lax.rem(x + 1, 4), y, z, c), dev(lax.rem(x + 3, 4), y, z, c)
    y_far = dev(x, lax.rem(y + 2, 4), z, c)
    partners = [along_z(r) for r in range(1, 8)]
    partners += [to_plane[1], to_plane[2], to_plane[3], from_plane[2]]
    partners += [x_right, x_left, y_far]

    sent = []

    def rcopy(src, dst, ss, rs, device):
        return pltpu.make_async_remote_copy(
            src_ref=src, dst_ref=dst, send_sem=ss, recv_sem=rs, device_id=device, device_id_type=MESH
        )

    def go(copy):
        copy.start()
        sent.append(copy)

    local = {}

    def lcopy(name, src, dst, i):
        local[name] = pltpu.make_async_copy(src, dst, loc_sem.at[i])
        local[name].start()

    lcopy("x", tok, ball.at[0, 0], 0)
    lcopy("m", meta, metall.at[0], 2)
    lcopy("wi", win.at[0], wi, 3)
    lcopy("wo", wout.at[0], wo, 4)
    lcopy("g", grd, ball.at[1, 0], 1)

    barrier = pltpu.get_barrier_semaphore()
    for p in partners:
        pl.semaphore_signal(barrier, inc=1, device_id=p, device_id_type=MESH)
    pl.semaphore_wait(barrier, len(partners))

    own = (tok, grd)

    def ag(a, d, h, half):
        rows = pl.ds(half * HALF, HALF)
        if h == 1:
            src = own[a].at[rows]
        else:
            src = ball.at[a, 8 - (h - 1) if d == 0 else h - 1, rows]
        dst = ball.at[a, 8 - h if d == 0 else h, rows]
        return rcopy(src, dst, ag_s.at[a, d, h - 1, half], ag_r.at[a, d, h - 1, half],
                     along_z(1 if d == 0 else 7))

    def ag_own(a):
        for i in range(2):
            go(ag(a, 0, 1, i))
            go(ag(a, 1, 1, 1 - i))

    def ag_relay(a, h, i):
        for d in range(2):
            half = d if i == 0 else 1 - d
            ag(a, d, h, half).wait_recv()
            if h < (4 if i == 0 else 3):
                go(ag(a, d, h + 1, half))

    def meta_copy(r):
        return rcopy(meta, metall.at[8 - r], meta_s.at[8 - r], meta_r.at[8 - r], along_z(r))

    ag_own(0)
    for r in (1, 7, 2, 6, 3, 5, 4):
        go(meta_copy(r))

    row = lax.broadcasted_iota(jnp.int32, (T, T), 0)
    q = lax.div(row, CAP)
    q_c = lax.rem(c + lax.rem(q, 2), 2)
    q_y = lax.rem(y_lo + lax.div(q, 2), 2)
    row_place = (((z * 2 + q_y) * 2 + q_c) * CAP + lax.rem(row, CAP)).astype(F32)

    def onehots(r):
        m = metall[r]
        return [jnp.where(m[k:k + 1, :] == row_place, 1.0, 0.0) for k in range(4)], m

    def build(r):
        if r == 0:
            local["m"].wait()
        else:
            meta_copy(8 - r).wait_recv()
        hots, m = onehots(r)
        total = hots[0] + hots[1] + hots[2] + hots[3]
        gated = sum(hots[k] * m[4 + k:5 + k, :] for k in range(4))
        sel[r] = total.astype(BF)
        selt[r] = total.T.astype(BF)
        gatet[r] = gated.T.astype(BF)
        gslot[r] = jnp.broadcast_to(jnp.sum(gated, axis=1, keepdims=True), (T, T))

    def disp_copy(a, r, k):
        p = POS[r]
        return rcopy(disp.at[a, p, k - 1], arr.at[a, p, k], disp_s.at[a, p, k], disp_r.at[a, p, k],
                     to_plane[k])

    def dispatch(a, r):
        if r == 0:
            local["x" if a == 0 else "g"].wait()
        rows = dot(sel[r], ball[a, r])
        if a == 1:
            rows = rows * gslot[r][:, 0:1]
        rows = rows.astype(BF)
        p = POS[r]
        for k in (2, 3, 1):
            disp[a, p, k - 1] = rows[k * CAP:(k + 1) * CAP]
            go(disp_copy(a, r, k))
        arr[a, p, 0] = rows[:CAP]

    def ret_copy(a, p, k):
        return rcopy(res.at[a, p, k], ret.at[a, p, k], ret_s.at[a, p, k], ret_r.at[a, p, k],
                     from_plane[k])

    def give_back(a, j):
        for p in (2 * j, 2 * j + 1):
            for k in (2, 3, 1):
                go(ret_copy(a, p, k))
            ret[a, p, 0] = res[a, p, 0]

    def await_rows(a, j):
        for p in (2 * j, 2 * j + 1):
            for k in (1, 2, 3):
                disp_copy(a, ORDER[p], k).wait_recv()

    def forward(j):
        await_rows(0, j)
        rows = arr[0, 2 * j:2 * j + 2].reshape(256, D)

        def tile(n, _):
            cols = pl.ds(pl.multiple_of(n * 256, 256), 256)
            v = dot(rows, wi[:, cols])
            half_one = 0.5 * (1.0 + lax.erf(v * ROOT_HALF))
            act[pl.ds(256 * j, 256), cols] = (v * half_one).astype(BF)
            slope[pl.ds(256 * j, 256), cols] = half_one + v * INV_ROOT_TAU * jnp.exp(-0.5 * v * v)
            return 0

        lax.fori_loop(0, 4, tile, 0)
        hidden = act[pl.ds(256 * j, 256), :]

        def tile_out(n, _):
            cols = pl.ds(pl.multiple_of(n * 256, 256), 256)
            res[0, 2 * j:2 * j + 2, :, :, cols] = (
                dot(hidden, wo[:, cols]).astype(BF).reshape(2, 4, CAP, 256)
            )
            return 0

        lax.fori_loop(0, 4, tile_out, 0)
        give_back(0, j)

    def backward(j):
        rows = arr[1, 2 * j:2 * j + 2].reshape(256, D)

        def tile(n, _):
            cols = pl.ds(pl.multiple_of(n * 256, 256), 256)
            v = dot(rows, wo[cols, :], ((1,), (1,)))
            pre[pl.ds(256 * j, 256), cols] = (v * slope[pl.ds(256 * j, 256), cols]).astype(BF)
            return 0

        lax.fori_loop(0, 4, tile, 0)
        hidden = pre[pl.ds(256 * j, 256), :]

        def tile_out(n, _):
            cols = pl.ds(pl.multiple_of(n * 256, 256), 256)
            res[1, 2 * j:2 * j + 2, :, :, cols] = (
                dot(hidden, wi[cols, :], ((1,), (1,))).astype(BF).reshape(2, 4, CAP, 256)
            )
            return 0

        lax.fori_loop(0, 4, tile_out, 0)
        give_back(1, j)

    returned = set()

    def combine(a, r, half):
        p = POS[r]
        if (a, p) not in returned:
            returned.add((a, p))
            for k in (1, 2, 3):
                ret_copy(a, p, k).wait_recv()
        weights = (gatet if a == 0 else selt)[r, half * HALF:(half + 1) * HALF]
        return dot(weights, ret[a, p].reshape(T, D))

    def rs_copy(a, d, i):
        return rcopy(rs_send.at[a, d, i], rs_recv.at[a, d, i], rs_s.at[a, d, i], rs_r.at[a, d, i],
                     along_z(1 if d == 0 else 7))

    def rs(a, i):
        for d in range(2):
            half, r = RS_UNITS[d][i]
            prior = (half, r + 1 if d == 0 else r - 1)
            total = combine(a, r, half)
            if prior in RS_UNITS[d]:
                n = RS_UNITS[d].index(prior)
                rs_copy(a, d, n).wait_recv()
                total = total + rs_recv[a, d, n].astype(F32)
            rs_send[a, d, i] = total.astype(BF)
            go(rs_copy(a, d, i))

    def rs_end(a, out):
        for half in range(2):
            total = combine(a, 0, half)
            for d in range(2):
                n = RS_UNITS[d].index((half, 1 if d == 0 else 7))
                rs_copy(a, d, n).wait_recv()
                total = total + rs_recv[a, d, n].astype(F32)
            out[half * HALF:(half + 1) * HALF, :] = total.astype(BF)

    def gg_copy(r):
        return rcopy(gg_send.at[r], gg_recv.at[r], gg_s.at[r], gg_r.at[r], along_z(r))

    def gate_grad(r):
        m = dot(ret[0, POS[r]].reshape(T, D), ball[1, r], ((1,), (1,)))
        hots, _ = onehots(r)
        out = gg_send if r else gg_recv
        for k in range(4):
            out[r, k:k + 1, :] = jnp.sum(m * hots[k], axis=0, keepdims=True)
        if r:
            out[r, 4:8, :] = jnp.zeros((4, T), F32)
            go(gg_copy(r))

    def wx_copy(w, i):
        return rcopy(wx_send.at[w, i], wx_recv.at[w, i], wx_s.at[w, i], wx_r.at[w, i],
                     x_right if i < 3 else x_left)

    def wgrad(w, dx):
        lhs_ref, rhs = (act, arr.at[1]) if w == 1 else (arr.at[0], pre)
        dest = lax.rem(x + dx, 4)
        parts = []
        for yh in range(2):
            cols = pl.ds(pl.multiple_of((yh * 4 + dest) * 128, 128), 128)
            if w == 1:
                parts.append(act[:, cols])
            else:
                parts.append(arr[0, :, :, :, cols].reshape(1024, 128))
        lhs = jnp.concatenate(parts, axis=1)

        def tile(n, _):
            cols = pl.ds(pl.multiple_of(n * 256, 256), 256)
            if w == 1:
                right = arr[1, :, :, :, cols].reshape(1024, 256)
            else:
                right = pre[:, cols]
            v = dot(lhs, right, ((0,), (0,)))
            a, b = v[:128], v[128:]
            if dx == 2:
                wx_send[w, 3, :, cols] = a.astype(BF)
                wx_send[w, 0, :, cols] = b.astype(BF)
            elif dx == 1:
                wx_send[w, 1, :, cols] = a.astype(BF)
                wx_chain[w, 0, :, cols] = b
            elif dx == 3:
                wx_send[w, 4, :, cols] = b.astype(BF)
                wx_chain[w, 1, :, cols] = a
            else:
                wx_own[w, 0, :, cols] = a
                wx_own[w, 1, :, cols] = b
            return 0

        lax.fori_loop(0, 4, tile, 0)
        for i in {2: (3, 0), 1: (1,), 3: (4,), 0: ()}[dx]:
            go(wx_copy(w, i))

    def wchain(w):
        for i, first, n in ((2, 0, 0), (5, 3, 1)):
            wx_copy(w, first).wait_recv()
            wx_send[w, i] = (wx_chain[w, n] + wx_recv[w, first].astype(F32)).astype(BF)
            go(wx_copy(w, i))

    def wy_copy(w):
        return rcopy(wy_send.at[w], wy_recv.at[w], wy_s.at[w], wy_r.at[w], y_far)

    def wsum(w):
        for i in (1, 2, 4, 5):
            wx_copy(w, i).wait_recv()
        wx_own[w, 0] = wx_own[w, 0] + wx_recv[w, 1].astype(F32) + wx_recv[w, 5].astype(F32)
        wx_own[w, 1] = wx_own[w, 1] + wx_recv[w, 2].astype(F32) + wx_recv[w, 4].astype(F32)
        wy_send[w] = wx_own[w, 1 - y_hi].astype(BF)
        go(wy_copy(w))

    def wend(w, out):
        wy_copy(w).wait_recv()
        out[...] = wx_own[w, y_hi] + wy_recv[w].astype(F32)

    build(0)
    dispatch(0, 0)
    ag_relay(0, 1, 0)
    ag_relay(0, 1, 1)
    build(7)
    build(1)
    dispatch(0, 7)
    dispatch(0, 1)
    ag_relay(0, 2, 0)
    local["wi"].wait()
    local["wo"].wait()
    forward(0)
    ag_relay(0, 2, 1)
    build(6)
    build(2)
    dispatch(0, 6)
    dispatch(0, 2)
    ag_relay(0, 3, 0)
    ag_own(1)
    forward(1)
    ag_relay(0, 3, 1)
    build(5)
    build(3)
    dispatch(0, 5)
    dispatch(0, 3)
    forward(2)
    ag_relay(0, 4, 0)
    build(4)
    dispatch(0, 4)
    dispatch(1, 0)
    ag_relay(1, 1, 0)
    forward(3)
    ag_relay(1, 1, 1)
    dispatch(1, 7)
    dispatch(1, 1)
    ag_relay(1, 2, 0)
    await_rows(1, 0)
    backward(0)
    ag_relay(1, 2, 1)
    dispatch(1, 6)
    dispatch(1, 2)
    ag_relay(1, 3, 0)
    rs(0, 0)
    rs(0, 1)
    await_rows(1, 1)
    backward(1)
    ag_relay(1, 3, 1)
    dispatch(1, 5)
    dispatch(1, 3)
    await_rows(1, 2)
    backward(2)
    ag_relay(1, 4, 0)
    dispatch(1, 4)
    await_rows(1, 3)
    wgrad(1, 2)
    rs(0, 2)
    wgrad(1, 1)
    wgrad(1, 3)
    rs(0, 3)
    backward(3)
    wgrad(1, 0)
    rs(0, 4)
    wgrad(0, 2)
    wchain(1)
    rs(0, 5)
    wgrad(0, 1)
    wgrad(0, 3)
    rs(0, 6)
    rs(1, 0)
    rs(1, 1)
    wgrad(0, 0)
    for r in (4, 3, 5, 2, 6, 1, 7, 0):
        if r == 0:
            combined = [combine(0, 0, 0)]
        gate_grad(r)
    wchain(0)
    rs(1, 2)
    rs_end(0, mixed_o)
    rs(1, 3)
    wsum(1)
    rs(1, 4)
    rs(1, 5)
    wsum(0)
    rs(1, 6)
    for r in range(1, 8):
        gg_copy(r).wait_recv()
    gg = gg_recv[0]
    for r in range(1, 8):
        gg = gg + gg_recv[r]
    gg_o[...] = gg
    wend(1, gout_o)
    rs_end(1, tgrad_o)
    wend(0, gin_o)
    for copy in sent:
        copy.wait_send()


def places(expert_ids):
    experts = jnp.arange(32, dtype=jnp.int32)
    hot = (expert_ids[:, :, None] == experts).astype(jnp.int32)
    named = jnp.sum(hot, axis=1)
    before = jnp.tril(jnp.ones((T, T), F32), -1) @ named.astype(F32)
    slot = jnp.sum(before[:, None, :] * hot.astype(F32), axis=2)
    return expert_ids.astype(F32) * CAP + slot


def body(tokens, expert_ids, gate_probs, out_grad, w_in, w_out):
    meta = jnp.concatenate([places(expert_ids).T, gate_probs.T], axis=0)
    anyspec = pl.BlockSpec(memory_space=pl.ANY)
    vmem = pl.BlockSpec(memory_space=pltpu.VMEM)
    dma = pltpu.SemaphoreType.DMA
    scratch = [
        pltpu.VMEM((2, 8, T, D), BF),
        pltpu.VMEM((8, 8, T), F32),
        pltpu.VMEM((8, T, T), BF),
        pltpu.VMEM((8, T, T), BF),
        pltpu.VMEM((8, T, T), BF),
        pltpu.VMEM((8, T, T), F32),
        pltpu.VMEM((D, D), BF),
        pltpu.VMEM((D, D), BF),
        pltpu.VMEM((2, 8, 3, CAP, D), BF),
        pltpu.VMEM((2, 8, 4, CAP, D), BF),
        pltpu.VMEM((1024, D), BF),
        pltpu.VMEM((1024, D), F32),
        pltpu.VMEM((1024, D), BF),
        pltpu.VMEM((2, 8, 4, CAP, D), BF),
        pltpu.VMEM((2, 8, 4, CAP, D), BF),
        pltpu.VMEM((2, 2, 7, HALF, D), BF),
        pltpu.VMEM((2, 2, 7, HALF, D), BF),
        pltpu.VMEM((8, 8, T), F32),
        pltpu.VMEM((8, 8, T), F32),
        pltpu.VMEM((2, 6, 128, D), BF),
        pltpu.VMEM((2, 6, 128, D), BF),
        pltpu.VMEM((2, 2, 128, D), F32),
        pltpu.VMEM((2, 2, 128, D), F32),
        pltpu.VMEM((2, 128, D), BF),
        pltpu.VMEM((2, 128, D), BF),
        dma((5,)),
        dma((2, 2, 4, 2)), dma((2, 2, 4, 2)),
        dma((8,)), dma((8,)),
        dma((2, 8, 4)), dma((2, 8, 4)),
        dma((2, 8, 4)), dma((2, 8, 4)),
        dma((2, 2, 7)), dma((2, 2, 7)),
        dma((8,)), dma((8,)),
        dma((2, 6)), dma((2, 6)),
        dma((2,)), dma((2,)),
    ]
    mixed, tgrad, gg, gin, gout = pl.pallas_call(
        kernel,
        out_shape=(
            jax.ShapeDtypeStruct((T, D), BF),
            jax.ShapeDtypeStruct((T, D), BF),
            jax.ShapeDtypeStruct((8, T), F32),
            jax.ShapeDtypeStruct((128, D), F32),
            jax.ShapeDtypeStruct((128, D), F32),
        ),
        in_specs=[anyspec] * 5,
        out_specs=(vmem,) * 5,
        scratch_shapes=scratch,
        compiler_params=pltpu.CompilerParams(
            collective_id=0, has_side_effects=True, vmem_limit_bytes=62 * 1024 * 1024
        ),
        cost_estimate=pl.CostEstimate(
            flops=14_000_000_000, bytes_accessed=8_000_000, transcendentals=2_000_000
        ),
    )(tokens, out_grad, meta, w_in, w_out)
    return mixed, tgrad, gg[:4].T, gin[None], gout[None]


def solution(mesh):
    token = P(("rep", "ep"), None)
    weight = P("ep", None, None)
    return jax.shard_map(
        body,
        mesh=mesh,
        in_specs=(token, token, token, token, weight, weight),
        out_specs=(token, token, token, P("ep", "rep", None), P("ep", "rep", None)),
        check_vma=False,
    )
```

time: 350 us -> 150 us (0.43)
  waiting for transfers between devices: 217 us -> 0 us
  Pallas kernels: 0 us -> 138 us
  matrix products: 34.9 us -> 0.2 us
  local copies, waits for them, and re-layouts: 40.2 us -> 7.33 us
  starting transfers between devices: 26.5 us -> 0 us
  between operations: 14.2 us -> 0.66 us
  other arithmetic: 15.7 us -> 3.4 us
    all_to_all x4 -> x0, waiting for transfers between devices: 147 us -> none  [the longest x1 44.1 us: body(): lax.all_to_all(g_sent, 'ep', split_axis=0, concat_axis=0, tiled=True)]
    pallas_call x0 -> x1, Pallas kernels: none -> 138 us  [body(): pl.pallas_call(kernel, out_shape=(jax.ShapeDtypeStruct((T, D), BF), jax.S...]
    unnamed x4 -> x0, waiting for transfers between devices: 70.1 us -> none
    dot_general x6 -> x1, matrix products: 34.9 us -> 0.2 us  [places(): before = jnp.tril(jnp.ones((T, T), F32), -1) @ named.astype(F32)]
    all_to_all x4 -> x0, starting transfers between devices: 26.2 us -> none  [the longest x1 11.3 us: body(): lax.all_to_all(x_sent, 'ep', split_axis=0, concat_axis=0, tiled=True)]
    gather x2 -> x0, local copies, waits for them, and re-layouts: 9.19 us -> none  [the longest x1 4.6 us: body(): picked_grad = grad_back.reshape(experts * capacity, features)[target]]
    unnamed x17 -> x6, local copies, waits for them, and re-layouts: 15.1 us -> 6.02 us
    reduce_sum x3 -> x2, other arithmetic: 7.55 us -> 1.43 us  [the longest x1 0.73 us: places(): slot = jnp.sum(before[:, None, :] * hot.astype(F32), axis=2)]
  transfers between devices with their start and end apart: 6 -> 0, of which waited for: 5 -> 0; matrix products, arithmetic and copies ran while one was open for 19% -> 0% of each run, Pallas kernels for 0% -> 0%
where the time goes in v1:
time: 150 us
  Pallas kernels  138 us (92%)
  local copies, waits for them, and re-layouts  7.33 us (5%)
  other arithmetic  3.4 us (2%)
    pallas_call x1, Pallas kernels, body(): pl.pallas_call(kernel, out_shape=(jax.ShapeDtypeStruct((T, D), BF), jax.S...  138 us
    unnamed x6, local copies, waits for them, and re-layouts  6.02 us

profile of v1, /device:TPU:1, one launch (start us, length us, event | category | flops | bytes accessed | tf_op | source)
XLA Modules:
  0.0 149.6 jit_solution(10797656774095771566)
XLA Ops:
  0.6 0.7 convert_reduce_fusion
  1.3 0.2 fusion.2
  1.5 0.7 fusion.1
  2.3 0.7 add_bitcast_fusion
  3.0 1.3 pad_maximum_fusion.meta
  4.2 138.0 %shard_map.101 = (bf16[128,1024]{1,0:T(8,128)(2,1)}, bf16[128,1024]{1,0:T(8,128)(2,1)}, f32[8,128]{1,0:T(8,128)}, f32[128,1024]{1,0:T(8,128)}, f32[128,1024]{1,0:T(8,128)}) custom-call(bf16[128,1024]{1,0:T(8,128)(2,1)} %tok.1, bf16[128,1024]{1,0:T(8,128)(2,1)} %grd.1, f32[8,128]{1,0:T(8,128)} %pad_maximum_fusion.meta, bf16[1,1024,1024]{2,1,0:T(8,128)(2,1)} %win.1, ...), custom_call_target="tpu_custom_call" | custom-call | flops 14000000000 | bytes 8000000 | tf_op jit(solution)/shard_map/pallas_call | solution.py:489
  142.2 0.0 copy-start
  142.2 1.3 slice_bitcast_fusion
  143.5 1.7 %copy.17 = bf16[128,1024]{1,0:T(8,128)(2,1)} copy(bf16[128,1024]{1,0:T(8,128)(2,1)} %get-tuple-element.20) | data formatting | bytes 524288
  145.2 1.7 %copy.18 = bf16[128,1024]{1,0:T(8,128)(2,1)} copy(bf16[128,1024]{1,0:T(8,128)(2,1)} %get-tuple-element.21) | data formatting | bytes 524288
  146.9 1.9 %copy.19 = f32[1,128,1024]{2,1,0:T(8,128)} copy(f32[1,128,1024]{2,1,0:T(8,128)} %bitcast.8) | data formatting | bytes 1048576
  148.8 0.0 copy-done
  148.8 0.8 copy.20
  (1 shorter events, 0.0 us)
Async XLA Ops:
  142.2 6.5 %copy-start = (f32[128,1024]{1,0:T(8,128)S(1)}, f32[128,1024]{1,0:T(8,128)}, u32[]{:S(2)}) copy-start(f32[128,1024]{1,0:T(8,128)} %get-tuple-element.14) | copy-start | bytes 1572868

commit v2 on v1

--- a/solution.py
+++ b/solution.py
@@ -13,8 +13,11 @@
 HALF = 64
 CAP = 32
 D = 1024
+LOG2_E = 1.4426950408889634
+INV_ROOT_TAU = 0.3989422804014327
+ERF_P = 0.3275911
+ERF_A = (0.254829592, -0.284496736, 1.421413741, -1.453152027, 1.061405429)
 ROOT_HALF = 0.7071067811865476
-INV_ROOT_TAU = 0.3989422804014327
 
 ORDER = (0, 7, 1, 6, 2, 5, 3, 4)
 POS = {r: p for p, r in enumerate(ORDER)}
@@ -28,11 +31,24 @@
     return lax.dot_general(a, b, (dims, ((), ())), preferred_element_type=F32)
 
 
+def gelu_parts(v):
+    bell = jnp.exp2(v * v * (-0.5 * LOG2_E))
+    base = 1.0 + jnp.abs(v) * (ERF_P * ROOT_HALF)
+    t = pl.reciprocal(base, approx=True)
+    t = t * (2.0 - base * t)
+    poly = 0.5 * ERF_A[4]
+    for a in ERF_A[3::-1]:
+        poly = poly * t + 0.5 * a
+    tail = poly * t * bell
+    return jnp.where(v < 0.0, tail, 1.0 - tail), v * bell * INV_ROOT_TAU
+
+
 def kernel(
-    tok, grd, meta, win, wout,
+    tok, grd, ids, gates, win, wout,
     mixed_o, tgrad_o, gg_o, gin_o, gout_o,
-    ball, metall, sel, selt, gatet, gslot, wi, wo,
-    disp, arr, act, slope, pre, res, ret,
+    ball, metall, sel, selt, gatet, gslot, wi, wo, wit, wot,
+    disp, arr, arrt, actt, slope, pre, res, ret,
+    mixed_v, tgrad_v, gg_v, gin_v, gout_v, hid,
     rs_send, rs_recv, gg_send, gg_recv,
     wx_send, wx_recv, wx_own, wx_chain, wy_send, wy_recv,
     loc_sem, ag_s, ag_r, meta_s, meta_r, disp_s, disp_r, ret_s, ret_r,
@@ -83,10 +99,12 @@
         local[name].start()
 
     lcopy("x", tok, ball.at[0, 0], 0)
-    lcopy("m", meta, metall.at[0], 2)
     lcopy("wi", win.at[0], wi, 3)
     lcopy("wo", wout.at[0], wo, 4)
     lcopy("g", grd, ball.at[1, 0], 1)
+
+    def out_copy(name, src, dst, i):
+        lcopy(name, src, dst, 5 + i)
 
     barrier = pltpu.get_barrier_semaphore()
     for p in partners:
@@ -118,9 +136,21 @@
                 go(ag(a, d, h + 1, half))
 
     def meta_copy(r):
-        return rcopy(meta, metall.at[8 - r], meta_s.at[8 - r], meta_r.at[8 - r], along_z(r))
+        return rcopy(metall.at[0], metall.at[8 - r], meta_s.at[8 - r], meta_r.at[8 - r], along_z(r))
 
     ag_own(0)
+
+    expert = lax.broadcasted_iota(jnp.int32, (32, T), 0)
+    named = [jnp.where(ids[k:k + 1, :] == expert, 1.0, 0.0) for k in range(4)]
+    earlier = jnp.where(
+        lax.broadcasted_iota(jnp.int32, (T, T), 0) < lax.broadcasted_iota(jnp.int32, (T, T), 1), 1.0, 0.0
+    ).astype(BF)
+    before = dot((named[0] + named[1] + named[2] + named[3]).astype(BF), earlier)
+    for k in range(4):
+        metall[0, k:k + 1, :] = (
+            ids[k:k + 1, :].astype(F32) * CAP + jnp.sum(named[k] * before, axis=0, keepdims=True)
+        )
+    metall[0, 4:8, :] = gates[...]
     for r in (1, 7, 2, 6, 3, 5, 4):
         go(meta_copy(r))
 
@@ -135,9 +165,7 @@
         return [jnp.where(m[k:k + 1, :] == row_place, 1.0, 0.0) for k in range(4)], m
 
     def build(r):
-        if r == 0:
-            local["m"].wait()
-        else:
+        if r:
             meta_copy(8 - r).wait_recv()
         hots, m = onehots(r)
         total = hots[0] + hots[1] + hots[2] + hots[3]
@@ -175,56 +203,61 @@
                 go(ret_copy(a, p, k))
             ret[a, p, 0] = res[a, p, 0]
 
+    awaited = set()
+
     def await_rows(a, j):
+        if (a, j) in awaited:
+            return
+        awaited.add((a, j))
         for p in (2 * j, 2 * j + 1):
             for k in (1, 2, 3):
                 disp_copy(a, ORDER[p], k).wait_recv()
 
-    def forward(j):
+    def turn_weights(n):
+        rows = pl.ds(n * 256, 256)
+        wit[:, rows] = wi[rows, :].T
+        wot[:, rows] = wo[rows, :].T
+
+    def forward_a(j):
         await_rows(0, j)
         rows = arr[0, 2 * j:2 * j + 2].reshape(256, D)
-
-        def tile(n, _):
-            cols = pl.ds(pl.multiple_of(n * 256, 256), 256)
+        span = pl.ds(256 * j, 256)
+        acts = []
+        for n in range(4):
+            cols = pl.ds(n * 256, 256)
             v = dot(rows, wi[:, cols])
-            half_one = 0.5 * (1.0 + lax.erf(v * ROOT_HALF))
-            act[pl.ds(256 * j, 256), cols] = (v * half_one).astype(BF)
-            slope[pl.ds(256 * j, 256), cols] = half_one + v * INV_ROOT_TAU * jnp.exp(-0.5 * v * v)
-            return 0
-
-        lax.fori_loop(0, 4, tile, 0)
-        hidden = act[pl.ds(256 * j, 256), :]
-
-        def tile_out(n, _):
-            cols = pl.ds(pl.multiple_of(n * 256, 256), 256)
+            below, dense = gelu_parts(v)
+            slope[span, cols] = below + dense
+            acts.append((v * below).astype(BF))
+            actt[cols, span] = acts[-1].T
+        hid[...] = jnp.concatenate(acts, axis=1)
+
+    def forward_b(j):
+        span = pl.ds(256 * j, 256)
+        hidden = hid[...]
+        for n in range(4):
+            cols = pl.ds(n * 256, 256)
             res[0, 2 * j:2 * j + 2, :, :, cols] = (
                 dot(hidden, wo[:, cols]).astype(BF).reshape(2, 4, CAP, 256)
             )
-            return 0
-
-        lax.fori_loop(0, 4, tile_out, 0)
         give_back(0, j)
-
-    def backward(j):
+        arrt[:, span] = arr[0, 2 * j:2 * j + 2].reshape(256, D).T
+
+    def backward_a(j):
+        await_rows(1, j)
         rows = arr[1, 2 * j:2 * j + 2].reshape(256, D)
-
-        def tile(n, _):
-            cols = pl.ds(pl.multiple_of(n * 256, 256), 256)
-            v = dot(rows, wo[cols, :], ((1,), (1,)))
-            pre[pl.ds(256 * j, 256), cols] = (v * slope[pl.ds(256 * j, 256), cols]).astype(BF)
-            return 0
-
-        lax.fori_loop(0, 4, tile, 0)
+        span = pl.ds(256 * j, 256)
+        for n in range(4):
+            cols = pl.ds(n * 256, 256)
+            pre[span, cols] = (dot(rows, wot[:, cols]) * slope[span, cols]).astype(BF)
+
+    def backward_b(j):
         hidden = pre[pl.ds(256 * j, 256), :]
-
-        def tile_out(n, _):
-            cols = pl.ds(pl.multiple_of(n * 256, 256), 256)
+        for n in range(4):
+            cols = pl.ds(n * 256, 256)
             res[1, 2 * j:2 * j + 2, :, :, cols] = (
-                dot(hidden, wi[cols, :], ((1,), (1,))).astype(BF).reshape(2, 4, CAP, 256)
+                dot(hidden, wit[:, cols]).astype(BF).reshape(2, 4, CAP, 256)
             )
-            return 0
-
-        lax.fori_loop(0, 4, tile_out, 0)
         give_back(1, j)
 
     returned = set()
@@ -281,24 +314,15 @@
                      x_right if i < 3 else x_left)
 
     def wgrad(w, dx):
-        lhs_ref, rhs = (act, arr.at[1]) if w == 1 else (arr.at[0], pre)
+        left = actt if w == 1 else arrt
         dest = lax.rem(x + dx, 4)
-        parts = []
-        for yh in range(2):
-            cols = pl.ds(pl.multiple_of((yh * 4 + dest) * 128, 128), 128)
-            if w == 1:
-                parts.append(act[:, cols])
-            else:
-                parts.append(arr[0, :, :, :, cols].reshape(1024, 128))
-        lhs = jnp.concatenate(parts, axis=1)
-
-        def tile(n, _):
-            cols = pl.ds(pl.multiple_of(n * 256, 256), 256)
-            if w == 1:
-                right = arr[1, :, :, :, cols].reshape(1024, 256)
-            else:
-                right = pre[:, cols]
-            v = dot(lhs, right, ((0,), (0,)))
+        lhs = jnp.concatenate(
+            [left[pl.ds(pl.multiple_of((yh * 4 + dest) * 128, 128), 128), :] for yh in range(2)], axis=0
+        )
+        for n in range(4):
+            cols = pl.ds(n * 256, 256)
+            right = arr[1, :, :, :, cols].reshape(1024, 256) if w == 1 else pre[:, cols]
+            v = dot(lhs, right)
             a, b = v[:128], v[128:]
             if dx == 2:
                 wx_send[w, 3, :, cols] = a.astype(BF)
@@ -312,9 +336,6 @@
             else:
                 wx_own[w, 0, :, cols] = a
                 wx_own[w, 1, :, cols] = b
-            return 0
-
-        lax.fori_loop(0, 4, tile, 0)
         for i in {2: (3, 0), 1: (1,), 3: (4,), 0: ()}[dx]:
             go(wx_copy(w, i))
 
@@ -341,112 +362,131 @@
 
     build(0)
     dispatch(0, 0)
+    local["wi"].wait()
+    local["wo"].wait()
+    turn_weights(0)
     ag_relay(0, 1, 0)
-    ag_relay(0, 1, 1)
     build(7)
     build(1)
+    turn_weights(1)
+    ag_relay(0, 1, 1)
     dispatch(0, 7)
     dispatch(0, 1)
+    turn_weights(2)
     ag_relay(0, 2, 0)
-    local["wi"].wait()
-    local["wo"].wait()
-    forward(0)
-    ag_relay(0, 2, 1)
     build(6)
     build(2)
+    turn_weights(3)
+    ag_relay(0, 2, 1)
     dispatch(0, 6)
     dispatch(0, 2)
+    forward_a(0)
     ag_relay(0, 3, 0)
     ag_own(1)
-    forward(1)
-    ag_relay(0, 3, 1)
+    forward_b(0)
     build(5)
     build(3)
+    ag_relay(0, 3, 1)
     dispatch(0, 5)
     dispatch(0, 3)
-    forward(2)
+    forward_a(1)
+    build(4)
     ag_relay(0, 4, 0)
-    build(4)
     dispatch(0, 4)
+    forward_b(1)
     dispatch(1, 0)
     ag_relay(1, 1, 0)
-    forward(3)
+    forward_a(2)
     ag_relay(1, 1, 1)
+    forward_b(2)
     dispatch(1, 7)
     dispatch(1, 1)
     ag_relay(1, 2, 0)
-    await_rows(1, 0)
-    backward(0)
+    forward_a(3)
     ag_relay(1, 2, 1)
+    forward_b(3)
     dispatch(1, 6)
     dispatch(1, 2)
     ag_relay(1, 3, 0)
-    rs(0, 0)
-    rs(0, 1)
-    await_rows(1, 1)
-    backward(1)
+    backward_a(0)
+    backward_b(0)
     ag_relay(1, 3, 1)
     dispatch(1, 5)
     dispatch(1, 3)
-    await_rows(1, 2)
-    backward(2)
+    backward_a(1)
+    backward_b(1)
     ag_relay(1, 4, 0)
     dispatch(1, 4)
+    rs(0, 0)
+    rs(0, 1)
+    backward_a(2)
+    backward_b(2)
+    rs(0, 2)
     await_rows(1, 3)
     wgrad(1, 2)
-    rs(0, 2)
+    rs(0, 3)
     wgrad(1, 1)
     wgrad(1, 3)
-    rs(0, 3)
-    backward(3)
+    rs(0, 4)
+    backward_a(3)
+    backward_b(3)
+    rs(0, 5)
+    wgrad(0, 2)
     wgrad(1, 0)
-    rs(0, 4)
-    wgrad(0, 2)
-    wchain(1)
-    rs(0, 5)
-    wgrad(0, 1)
-    wgrad(0, 3)
     rs(0, 6)
     rs(1, 0)
     rs(1, 1)
+    wchain(1)
+    wgrad(0, 1)
+    wgrad(0, 3)
+    rs_end(0, mixed_v)
+    out_copy("mixed", mixed_v, mixed_o, 0)
+    rs(1, 2)
     wgrad(0, 0)
-    for r in (4, 3, 5, 2, 6, 1, 7, 0):
-        if r == 0:
-            combined = [combine(0, 0, 0)]
+    for r in (4, 3, 5, 2):
+        gate_grad(r)
+    rs(1, 3)
+    for r in (6, 1, 7, 0):
         gate_grad(r)
     wchain(0)
-    rs(1, 2)
-    rs_end(0, mixed_o)
-    rs(1, 3)
     wsum(1)
     rs(1, 4)
     rs(1, 5)
-    wsum(0)
-    rs(1, 6)
     for r in range(1, 8):
         gg_copy(r).wait_recv()
-    gg = gg_recv[0]
+    gg = gg_recv[0, 0:4, :]
     for r in range(1, 8):
-        gg = gg + gg_recv[r]
-    gg_o[...] = gg
-    wend(1, gout_o)
-    rs_end(1, tgrad_o)
-    wend(0, gin_o)
+        gg = gg + gg_recv[r, 0:4, :]
+    gg_v[...] = gg
+    out_copy("gg", gg_v, gg_o, 2)
+    rs(1, 6)
+    wend(1, gout_v)
+    out_copy("gout", gout_v, gout_o, 4)
+    wsum(0)
+    rs_end(1, tgrad_v)
+    out_copy("tgrad", tgrad_v, tgrad_o, 1)
+    wend(0, gin_v)
+    out_copy("gin", gin_v, gin_o, 3)
     for copy in sent:
         copy.wait_send()
-
-
-def places(expert_ids):
-    experts = jnp.arange(32, dtype=jnp.int32)
-    hot = (expert_ids[:, :, None] == experts).astype(jnp.int32)
-    named = jnp.sum(hot, axis=1)
-    before = jnp.tril(jnp.ones((T, T), F32), -1) @ named.astype(F32)
-    slot = jnp.sum(before[:, None, :] * hot.astype(F32), axis=2)
-    return expert_ids.astype(F32) * CAP + slot
+    for name in ("mixed", "gg", "gout", "tgrad", "gin"):
+        local[name].wait()
+
+
+def hand_on(*refs):
+    ins, outs, vms, sems = refs[:5], refs[5:10], refs[10:15], refs[15]
+    loads = [pltpu.make_async_copy(ins[i], vms[i], sems.at[0, i]) for i in range(5)]
+    stores = [pltpu.make_async_copy(vms[i], outs[i], sems.at[1, i]) for i in range(5)]
+    for load in loads:
+        load.start()
+    for load, store in zip(loads, stores):
+        load.wait()
+        store.start()
+    for store in stores:
+        store.wait()
 
 
 def body(tokens, expert_ids, gate_probs, out_grad, w_in, w_out):
-    meta = jnp.concatenate([places(expert_ids).T, gate_probs.T], axis=0)
     anyspec = pl.BlockSpec(memory_space=pl.ANY)
     vmem = pl.BlockSpec(memory_space=pltpu.VMEM)
     dma = pltpu.SemaphoreType.DMA
@@ -459,13 +499,22 @@
         pltpu.VMEM((8, T, T), F32),
         pltpu.VMEM((D, D), BF),
         pltpu.VMEM((D, D), BF),
+        pltpu.VMEM((D, D), BF),
+        pltpu.VMEM((D, D), BF),
         pltpu.VMEM((2, 8, 3, CAP, D), BF),
         pltpu.VMEM((2, 8, 4, CAP, D), BF),
-        pltpu.VMEM((1024, D), BF),
+        pltpu.VMEM((D, 1024), BF),
+        pltpu.VMEM((D, 1024), BF),
         pltpu.VMEM((1024, D), F32),
         pltpu.VMEM((1024, D), BF),
         pltpu.VMEM((2, 8, 4, CAP, D), BF),
         pltpu.VMEM((2, 8, 4, CAP, D), BF),
+        pltpu.VMEM((T, D), BF),
+        pltpu.VMEM((T, D), BF),
+        pltpu.VMEM((4, T), F32),
+        pltpu.VMEM((128, D), F32),
+        pltpu.VMEM((128, D), F32),
+        pltpu.VMEM((256, D), BF),
         pltpu.VMEM((2, 2, 7, HALF, D), BF),
         pltpu.VMEM((2, 2, 7, HALF, D), BF),
         pltpu.VMEM((8, 8, T), F32),
@@ -476,7 +525,7 @@
         pltpu.VMEM((2, 2, 128, D), F32),
         pltpu.VMEM((2, 128, D), BF),
         pltpu.VMEM((2, 128, D), BF),
-        dma((5,)),
+        dma((10,)),
         dma((2, 2, 4, 2)), dma((2, 2, 4, 2)),
         dma((8,)), dma((8,)),
         dma((2, 8, 4)), dma((2, 8, 4)),
@@ -486,26 +535,34 @@
         dma((2, 6)), dma((2, 6)),
         dma((2,)), dma((2,)),
     ]
-    mixed, tgrad, gg, gin, gout = pl.pallas_call(
+    shapes = (
+        jax.ShapeDtypeStruct((T, D), BF),
+        jax.ShapeDtypeStruct((T, D), BF),
+        jax.ShapeDtypeStruct((4, T), F32),
+        jax.ShapeDtypeStruct((128, D), F32),
+        jax.ShapeDtypeStruct((128, D), F32),
+    )
+    results = pl.pallas_call(
         kernel,
-        out_shape=(
-            jax.ShapeDtypeStruct((T, D), BF),
-            jax.ShapeDtypeStruct((T, D), BF),
-            jax.ShapeDtypeStruct((8, T), F32),
-            jax.ShapeDtypeStruct((128, D), F32),
-            jax.ShapeDtypeStruct((128, D), F32),
-        ),
-        in_specs=[anyspec] * 5,
-        out_specs=(vmem,) * 5,
+        out_shape=shapes,
+        in_specs=[anyspec] * 2 + [vmem] * 2 + [anyspec] * 2,
+        out_specs=(anyspec,) * 5,
         scratch_shapes=scratch,
         compiler_params=pltpu.CompilerParams(
-            collective_id=0, has_side_effects=True, vmem_limit_bytes=62 * 1024 * 1024
+            collective_id=0, has_side_effects=True, vmem_limit_bytes=63 * 1024 * 1024
         ),
         cost_estimate=pl.CostEstimate(
             flops=14_000_000_000, bytes_accessed=8_000_000, transcendentals=2_000_000
         ),
-    )(tokens, out_grad, meta, w_in, w_out)
-    return mixed, tgrad, gg[:4].T, gin[None], gout[None]
+    )(tokens, out_grad, expert_ids.T, gate_probs.T, w_in, w_out)
+    mixed, tgrad, gg, gin, gout = pl.pallas_call(
+        hand_on,
+        out_shape=shapes,
+        in_specs=[anyspec] * 5,
+        out_specs=(anyspec,) * 5,
+        scratch_shapes=[pltpu.VMEM(shape.shape, shape.dtype) for shape in shapes] + [dma((2, 5))],
+    )(*results)
+    return mixed, tgrad, gg.T, gin[None], gout[None]
 
 
 def solution(mesh):

time: 150 us -> 119 us (0.79)
  Pallas kernels: 138 us -> 118 us
  local copies, waits for them, and re-layouts: 7.33 us -> 0 us
  other arithmetic: 3.4 us -> 0 us
    pallas_call x1 -> x2, Pallas kernels: 138 us -> 118 us  [the longest x1 116 us: body(): pl.pallas_call(kernel, out_shape=shapes, in_specs=[anyspec] * 2 + [vmem]...]
    unnamed x6 -> x0, local copies, waits for them, and re-layouts: 6.02 us -> none
where the time goes in v2:
time: 119 us
  Pallas kernels  118 us (99%)
    pallas_call x1, Pallas kernels, body(): pl.pallas_call(kernel, out_shape=shapes, in_specs=[anyspec] * 2 + [vmem]...  116 us

profile of v2, /device:TPU:1, one launch (start us, length us, event | category | flops | bytes accessed | tf_op | source)
XLA Modules:
  0.0 118.7 jit_solution(1133945099933589825)
XLA Ops:
  0.6 115.6 %shard_map.101 = (bf16[128,1024]{1,0:T(8,128)(2,1)}, bf16[128,1024]{1,0:T(8,128)(2,1)}, f32[4,128]{1,0:T(4,128)}, f32[128,1024]{1,0:T(8,128)}, f32[128,1024]{1,0:T(8,128)}) custom-call(bf16[128,1024]{1,0:T(8,128)(2,1)} %tok.1, bf16[128,1024]{1,0:T(8,128)(2,1)} %grd.1, s32[4,128]{1,0:T(4,128)} %bitcast.7, f32[4,128]{1,0:T(4,128)} %bitcast.8, ...), custom_call_target="tpu_custom_call" | custom-call | flops 14000000000 | bytes 8000000 | tf_op jit(solution)/shard_map/pallas_call | solution.py:545
  116.2 2.3 %shard_map.102 = (bf16[128,1024]{1,0:T(8,128)(2,1)}, bf16[128,1024]{1,0:T(8,128)(2,1)}, f32[4,128]{1,0:T(4,128)}, f32[128,1024]{1,0:T(8,128)}, f32[128,1024]{1,0:T(8,128)}) custom-call(bf16[128,1024]{1,0:T(8,128)(2,1)} %get-tuple-element.15.refs_0_, bf16[128,1024]{1,0:T(8,128)(2,1)} %get-tuple-element.16.refs_1_, f32[4,128]{1,0:T(4,128)} %get-tuple-element.17.refs_2_, ...), custom_call_target="tpu_custom_call" | custom-call | tf_op jit(solution)/shard_map/pallas_call | solution.py:558

commit v3 on v2

--- a/solution.py
+++ b/solution.py
@@ -77,11 +77,9 @@
     )
     x_right, x_left = dev(lax.rem(x + 1, 4), y, z, c), dev(lax.rem(x + 3, 4), y, z, c)
     y_far = dev(x, lax.rem(y + 2, 4), z, c)
-    partners = [along_z(r) for r in range(1, 8)]
+    partners = [along_z(1), along_z(7)]
     partners += [to_plane[1], to_plane[2], to_plane[3], from_plane[2]]
-    partners += [x_right, x_left, y_far]
-
-    sent = []
+    partners += [x_right, x_left]
 
     def rcopy(src, dst, ss, rs, device):
         return pltpu.make_async_remote_copy(
@@ -90,7 +88,6 @@
 
     def go(copy):
         copy.start()
-        sent.append(copy)
 
     local = {}
 
@@ -120,7 +117,7 @@
         else:
             src = ball.at[a, 8 - (h - 1) if d == 0 else h - 1, rows]
         dst = ball.at[a, 8 - h if d == 0 else h, rows]
-        return rcopy(src, dst, ag_s.at[a, d, h - 1, half], ag_r.at[a, d, h - 1, half],
+        return rcopy(src, dst, ag_s.at[0], ag_r.at[a, h - 1, 0 if half == d else 1],
                      along_z(1 if d == 0 else 7))
 
     def ag_own(a):
@@ -129,14 +126,21 @@
             go(ag(a, 1, 1, 1 - i))
 
     def ag_relay(a, h, i):
+        rcopy(ball.at[a, 0], ball.at[a, 0], ag_s.at[0], ag_r.at[a, h - 1, i], along_z(1)).wait_recv()
         for d in range(2):
-            half = d if i == 0 else 1 - d
-            ag(a, d, h, half).wait_recv()
             if h < (4 if i == 0 else 3):
-                go(ag(a, d, h + 1, half))
-
-    def meta_copy(r):
-        return rcopy(metall.at[0], metall.at[8 - r], meta_s.at[8 - r], meta_r.at[8 - r], along_z(r))
+                go(ag(a, d, h + 1, d if i == 0 else 1 - d))
+
+    def meta_copy(d, h):
+        src, dst = (8 - (h - 1), 8 - h) if d == 0 else (h - 1, h)
+        return rcopy(metall.at[src % 8], metall.at[dst], meta_s.at[0], meta_r.at[d, h - 1],
+                     along_z(1 if d == 0 else 7))
+
+    def meta_relay(h):
+        for d in range(2 if h < 4 else 1):
+            meta_copy(d, h).wait_recv()
+            if h < (4 if d == 0 else 3):
+                go(meta_copy(d, h + 1))
 
     ag_own(0)
 
@@ -151,8 +155,8 @@
             ids[k:k + 1, :].astype(F32) * CAP + jnp.sum(named[k] * before, axis=0, keepdims=True)
         )
     metall[0, 4:8, :] = gates[...]
-    for r in (1, 7, 2, 6, 3, 5, 4):
-        go(meta_copy(r))
+    for d in range(2):
+        go(meta_copy(d, 1))
 
     row = lax.broadcasted_iota(jnp.int32, (T, T), 0)
     q = lax.div(row, CAP)
@@ -165,8 +169,6 @@
         return [jnp.where(m[k:k + 1, :] == row_place, 1.0, 0.0) for k in range(4)], m
 
     def build(r):
-        if r:
-            meta_copy(8 - r).wait_recv()
         hots, m = onehots(r)
         total = hots[0] + hots[1] + hots[2] + hots[3]
         gated = sum(hots[k] * m[4 + k:5 + k, :] for k in range(4))
@@ -177,7 +179,7 @@
 
     def disp_copy(a, r, k):
         p = POS[r]
-        return rcopy(disp.at[a, p, k - 1], arr.at[a, p, k], disp_s.at[a, p, k], disp_r.at[a, p, k],
+        return rcopy(disp.at[a, p, k - 1], arr.at[a, p, k], disp_s.at[0], disp_r.at[a, p // 2],
                      to_plane[k])
 
     def dispatch(a, r):
@@ -194,7 +196,7 @@
         arr[a, p, 0] = rows[:CAP]
 
     def ret_copy(a, p, k):
-        return rcopy(res.at[a, p, k], ret.at[a, p, k], ret_s.at[a, p, k], ret_r.at[a, p, k],
+        return rcopy(res.at[a, p, k], ret.at[a, p, k], ret_s.at[0], ret_r.at[a, p],
                      from_plane[k])
 
     def give_back(a, j):
@@ -209,9 +211,8 @@
         if (a, j) in awaited:
             return
         awaited.add((a, j))
-        for p in (2 * j, 2 * j + 1):
-            for k in (1, 2, 3):
-                disp_copy(a, ORDER[p], k).wait_recv()
+        two = disp.at[a, 2 * j:2 * j + 2]
+        rcopy(two, two, disp_s.at[0], disp_r.at[a, j], to_plane[1]).wait_recv()
 
     def turn_weights(n):
         rows = pl.ds(n * 256, 256)
@@ -258,7 +259,6 @@
             res[1, 2 * j:2 * j + 2, :, :, cols] = (
                 dot(hidden, wit[:, cols]).astype(BF).reshape(2, 4, CAP, 256)
             )
-        give_back(1, j)
 
     returned = set()
 
@@ -266,38 +266,41 @@
         p = POS[r]
         if (a, p) not in returned:
             returned.add((a, p))
-            for k in (1, 2, 3):
-                ret_copy(a, p, k).wait_recv()
+            rcopy(disp.at[a, p], disp.at[a, p], ret_s.at[0], ret_r.at[a, p], to_plane[1]).wait_recv()
         weights = (gatet if a == 0 else selt)[r, half * HALF:(half + 1) * HALF]
         return dot(weights, ret[a, p].reshape(T, D))
 
     def rs_copy(a, d, i):
-        return rcopy(rs_send.at[a, d, i], rs_recv.at[a, d, i], rs_s.at[a, d, i], rs_r.at[a, d, i],
+        return rcopy(rs_send.at[a, d, i], rs_recv.at[a, d, i], rs_s.at[0], rs_r.at[a, i],
                      along_z(1 if d == 0 else 7))
 
+    def rs_await(a, n):
+        rcopy(ball.at[a, 0], ball.at[a, 0], rs_s.at[0], rs_r.at[a, n], along_z(1)).wait_recv()
+
     def rs(a, i):
+        if i >= 2:
+            rs_await(a, i - 2)
         for d in range(2):
             half, r = RS_UNITS[d][i]
             prior = (half, r + 1 if d == 0 else r - 1)
             total = combine(a, r, half)
             if prior in RS_UNITS[d]:
-                n = RS_UNITS[d].index(prior)
-                rs_copy(a, d, n).wait_recv()
-                total = total + rs_recv[a, d, n].astype(F32)
+                total = total + rs_recv[a, d, i - 2].astype(F32)
             rs_send[a, d, i] = total.astype(BF)
             go(rs_copy(a, d, i))
 
     def rs_end(a, out):
+        rs_await(a, 5)
+        rs_await(a, 6)
         for half in range(2):
             total = combine(a, 0, half)
             for d in range(2):
                 n = RS_UNITS[d].index((half, 1 if d == 0 else 7))
-                rs_copy(a, d, n).wait_recv()
                 total = total + rs_recv[a, d, n].astype(F32)
             out[half * HALF:(half + 1) * HALF, :] = total.astype(BF)
 
     def gg_copy(r):
-        return rcopy(gg_send.at[r], gg_recv.at[r], gg_s.at[r], gg_r.at[r], along_z(r))
+        return rcopy(gg_send.at[r], gg_recv.at[r], gg_s.at[0], gg_r.at[0], along_z(r))
 
     def gate_grad(r):
         m = dot(ret[0, POS[r]].reshape(T, D), ball[1, r], ((1,), (1,)))
@@ -310,55 +313,67 @@
             go(gg_copy(r))
 
     def wx_copy(w, i):
-        return rcopy(wx_send.at[w, i], wx_recv.at[w, i], wx_s.at[w, i], wx_r.at[w, i],
+        return rcopy(wx_send.at[w, i], wx_recv.at[w, i], wx_s.at[0], wx_r.at[w, i],
                      x_right if i < 3 else x_left)
 
     def wgrad(w, dx):
         left = actt if w == 1 else arrt
         dest = lax.rem(x + dx, 4)
         lhs = jnp.concatenate(
-            [left[pl.ds(pl.multiple_of((yh * 4 + dest) * 128, 128), 128), :] for yh in range(2)], axis=0
+            [left[pl.ds(pl.multiple_of((yh * 4 + dest) * 128, 128), 128), :] for yh in (1 - y_hi, y_hi)],
+            axis=0,
         )
         for n in range(4):
             cols = pl.ds(n * 256, 256)
             right = arr[1, :, :, :, cols].reshape(1024, 256) if w == 1 else pre[:, cols]
             v = dot(lhs, right)
-            a, b = v[:128], v[128:]
+            far, near = v[:128], v[128:]
             if dx == 2:
-                wx_send[w, 3, :, cols] = a.astype(BF)
-                wx_send[w, 0, :, cols] = b.astype(BF)
+                wx_send[w, 0, :, cols] = far.astype(BF)
+                wx_send[w, 3, :, cols] = near.astype(BF)
             elif dx == 1:
-                wx_send[w, 1, :, cols] = a.astype(BF)
-                wx_chain[w, 0, :, cols] = b
+                wx_send[w, 1, :, cols] = near.astype(BF)
+                wx_chain[w, 0, :, cols] = far
             elif dx == 3:
-                wx_send[w, 4, :, cols] = b.astype(BF)
-                wx_chain[w, 1, :, cols] = a
+                wx_send[w, 4, :, cols] = far.astype(BF)
+                wx_chain[w, 1, :, cols] = near
             else:
-                wx_own[w, 0, :, cols] = a
-                wx_own[w, 1, :, cols] = b
-        for i in {2: (3, 0), 1: (1,), 3: (4,), 0: ()}[dx]:
-            go(wx_copy(w, i))
-
-    def wchain(w):
-        for i, first, n in ((2, 0, 0), (5, 3, 1)):
-            wx_copy(w, first).wait_recv()
-            wx_send[w, i] = (wx_chain[w, n] + wx_recv[w, first].astype(F32)).astype(BF)
-            go(wx_copy(w, i))
+                wx_own[w, 0, :, cols] = far
+                wx_own[w, 1, :, cols] = near
+
+    def wsend(w, i):
+        go(wx_copy(w, i))
+
+    def wchain(w, n):
+        i, first = (2, 0) if n == 0 else (5, 3)
+        wx_copy(w, first).wait_recv()
+        wx_send[w, i] = (wx_chain[w, n] + wx_recv[w, first].astype(F32)).astype(BF)
+        go(wx_copy(w, i))
 
     def wy_copy(w):
-        return rcopy(wy_send.at[w], wy_recv.at[w], wy_s.at[w], wy_r.at[w], y_far)
-
-    def wsum(w):
-        for i in (1, 2, 4, 5):
+        return rcopy(wy_send.at[w], wy_recv.at[w], wy_s.at[0], wy_r.at[w], y_far)
+
+    def wfar(w):
+        for i in (2, 4):
             wx_copy(w, i).wait_recv()
-        wx_own[w, 0] = wx_own[w, 0] + wx_recv[w, 1].astype(F32) + wx_recv[w, 5].astype(F32)
-        wx_own[w, 1] = wx_own[w, 1] + wx_recv[w, 2].astype(F32) + wx_recv[w, 4].astype(F32)
-        wy_send[w] = wx_own[w, 1 - y_hi].astype(BF)
+        total = wx_own[w, 0] + wx_recv[w, 2].astype(F32) + wx_recv[w, 4].astype(F32)
+        wy_send[w] = total.astype(BF)
         go(wy_copy(w))
 
     def wend(w, out):
+        for i in (1, 5):
+            wx_copy(w, i).wait_recv()
+        total = wx_own[w, 1] + wx_recv[w, 1].astype(F32) + wx_recv[w, 5].astype(F32)
         wy_copy(w).wait_recv()
-        out[...] = wx_own[w, y_hi] + wy_recv[w].astype(F32)
+        out[...] = total + wy_recv[w].astype(F32)
+
+    def backward(j):
+        backward_a(j)
+        backward_b(j)
+
+    def forward(j):
+        forward_a(j)
+        forward_b(j)
 
     build(0)
     dispatch(0, 0)
@@ -366,94 +381,109 @@
     local["wo"].wait()
     turn_weights(0)
     ag_relay(0, 1, 0)
+    meta_relay(1)
     build(7)
     build(1)
-    turn_weights(1)
+    dispatch(1, 0)
     ag_relay(0, 1, 1)
     dispatch(0, 7)
     dispatch(0, 1)
-    turn_weights(2)
+    turn_weights(1)
     ag_relay(0, 2, 0)
+    meta_relay(2)
     build(6)
     build(2)
-    turn_weights(3)
+    turn_weights(2)
     ag_relay(0, 2, 1)
     dispatch(0, 6)
     dispatch(0, 2)
     forward_a(0)
     ag_relay(0, 3, 0)
     ag_own(1)
-    forward_b(0)
+    meta_relay(3)
     build(5)
     build(3)
+    forward_b(0)
     ag_relay(0, 3, 1)
     dispatch(0, 5)
     dispatch(0, 3)
-    forward_a(1)
+    meta_relay(4)
     build(4)
+    forward(1)
     ag_relay(0, 4, 0)
     dispatch(0, 4)
-    forward_b(1)
-    dispatch(1, 0)
+    turn_weights(3)
     ag_relay(1, 1, 0)
-    forward_a(2)
+    forward(2)
     ag_relay(1, 1, 1)
-    forward_b(2)
     dispatch(1, 7)
     dispatch(1, 1)
+    forward(3)
     ag_relay(1, 2, 0)
-    forward_a(3)
     ag_relay(1, 2, 1)
-    forward_b(3)
     dispatch(1, 6)
     dispatch(1, 2)
+    backward(0)
     ag_relay(1, 3, 0)
-    backward_a(0)
-    backward_b(0)
+    rs(0, 0)
+    rs(0, 1)
+    backward(1)
     ag_relay(1, 3, 1)
     dispatch(1, 5)
     dispatch(1, 3)
-    backward_a(1)
-    backward_b(1)
     ag_relay(1, 4, 0)
     dispatch(1, 4)
-    rs(0, 0)
-    rs(0, 1)
-    backward_a(2)
-    backward_b(2)
+    give_back(1, 0)
+    give_back(1, 1)
+    backward(2)
+    give_back(1, 2)
     rs(0, 2)
     await_rows(1, 3)
     wgrad(1, 2)
+    wsend(1, 0)
+    wgrad(1, 3)
+    wsend(1, 4)
     rs(0, 3)
+    backward(3)
+    give_back(1, 3)
+    rs(0, 4)
+    wgrad(0, 2)
+    wsend(0, 0)
+    wgrad(0, 3)
+    wsend(0, 4)
+    wsend(1, 3)
+    rs(0, 5)
     wgrad(1, 1)
-    wgrad(1, 3)
-    rs(0, 4)
-    backward_a(3)
-    backward_b(3)
-    rs(0, 5)
-    wgrad(0, 2)
-    wgrad(1, 0)
+    wchain(1, 0)
+    wsend(0, 3)
     rs(0, 6)
     rs(1, 0)
     rs(1, 1)
-    wchain(1)
     wgrad(0, 1)
-    wgrad(0, 3)
+    wchain(0, 0)
+    wsend(1, 1)
+    wsend(0, 1)
+    wgrad(1, 0)
     rs_end(0, mixed_v)
     out_copy("mixed", mixed_v, mixed_o, 0)
+    wgrad(0, 0)
+    for r in (4, 3):
+        gate_grad(r)
     rs(1, 2)
-    wgrad(0, 0)
-    for r in (4, 3, 5, 2):
+    wchain(1, 1)
+    wfar(1)
+    for r in (5, 2):
         gate_grad(r)
     rs(1, 3)
-    for r in (6, 1, 7, 0):
+    wchain(0, 1)
+    for r in (6, 1):
         gate_grad(r)
-    wchain(0)
-    wsum(1)
     rs(1, 4)
+    wfar(0)
+    for r in (7, 0):
+        gate_grad(r)
     rs(1, 5)
-    for r in range(1, 8):
-        gg_copy(r).wait_recv()
+    rcopy(gg_send.at[1:8], gg_recv.at[1:8], gg_s.at[0], gg_r.at[0], along_z(1)).wait_recv()
     gg = gg_recv[0, 0:4, :]
     for r in range(1, 8):
         gg = gg + gg_recv[r, 0:4, :]
@@ -462,13 +492,15 @@
     rs(1, 6)
     wend(1, gout_v)
     out_copy("gout", gout_v, gout_o, 4)
-    wsum(0)
     rs_end(1, tgrad_v)
     out_copy("tgrad", tgrad_v, tgrad_o, 1)
     wend(0, gin_v)
     out_copy("gin", gin_v, gin_o, 3)
-    for copy in sent:
-        copy.wait_send()
+    for ref, sem in (
+        (rs_send, ag_s), (metall.at[1:8], meta_s), (disp, disp_s), (disp, ret_s), (rs_send, rs_s),
+        (gg_send.at[1:8], gg_s), (wx_send, wx_s), (wy_send, wy_s),
+    ):
+        rcopy(ref, ref, sem.at[0], wy_r.at[0], y_far).wait_send()
     for name in ("mixed", "gg", "gout", "tgrad", "gin"):
         local[name].wait()
 
@@ -526,14 +558,14 @@
         pltpu.VMEM((2, 128, D), BF),
         pltpu.VMEM((2, 128, D), BF),
         dma((10,)),
-        dma((2, 2, 4, 2)), dma((2, 2, 4, 2)),
-        dma((8,)), dma((8,)),
-        dma((2, 8, 4)), dma((2, 8, 4)),
-        dma((2, 8, 4)), dma((2, 8, 4)),
-        dma((2, 2, 7)), dma((2, 2, 7)),
-        dma((8,)), dma((8,)),
-        dma((2, 6)), dma((2, 6)),
-        dma((2,)), dma((2,)),
+        dma((1,)), dma((2, 4, 2)),
+        dma((1,)), dma((2, 4)),
+        dma((1,)), dma((2, 4)),
+        dma((1,)), dma((2, 8)),
+        dma((1,)), dma((2, 7)),
+        dma((1,)), dma((1,)),
+        dma((1,)), dma((2, 6)),
+        dma((1,)), dma((2,)),
     ]
     shapes = (
         jax.ShapeDtypeStruct((T, D), BF),

time: 119 us -> 112 us (0.941)
  Pallas kernels: 118 us -> 111 us
    pallas_call x1, Pallas kernels: 116 us -> 109 us  [body(): pl.pallas_call(kernel, out_shape=shapes, in_specs=[anyspec] * 2 + [vmem]...]
where the time goes in v3:
time: 112 us
  Pallas kernels  111 us (99%)
    pallas_call x1, Pallas kernels, body(): pl.pallas_call(kernel, out_shape=shapes, in_specs=[anyspec] * 2 + [vmem]...  109 us
    pallas_call x1, Pallas kernels, body(): pl.pallas_call(hand_on, out_shape=shapes, in_specs=[anyspec] * 5, out_spe...  2.26 us

profile of v3, /device:TPU:1, one launch (start us, length us, event | category | flops | bytes accessed | tf_op | source)
XLA Modules:
  0.0 111.8 jit_solution(3094664054566538950)
XLA Ops:
  0.6 108.7 %shard_map.101 = (bf16[128,1024]{1,0:T(8,128)(2,1)}, bf16[128,1024]{1,0:T(8,128)(2,1)}, f32[4,128]{1,0:T(4,128)}, f32[128,1024]{1,0:T(8,128)}, f32[128,1024]{1,0:T(8,128)}) custom-call(bf16[128,1024]{1,0:T(8,128)(2,1)} %tok.1, bf16[128,1024]{1,0:T(8,128)(2,1)} %grd.1, s32[4,128]{1,0:T(4,128)} %bitcast.7, f32[4,128]{1,0:T(4,128)} %bitcast.8, ...), custom_call_target="tpu_custom_call" | custom-call | flops 14000000000 | bytes 8000000 | tf_op jit(solution)/shard_map/pallas_call | solution.py:577
  109.4 2.3 %shard_map.102 = (bf16[128,1024]{1,0:T(8,128)(2,1)}, bf16[128,1024]{1,0:T(8,128)(2,1)}, f32[4,128]{1,0:T(4,128)}, f32[128,1024]{1,0:T(8,128)}, f32[128,1024]{1,0:T(8,128)}) custom-call(bf16[128,1024]{1,0:T(8,128)(2,1)} %get-tuple-element.15.refs_0_, bf16[128,1024]{1,0:T(8,128)(2,1)} %get-tuple-element.16.refs_1_, f32[4,128]{1,0:T(4,128)} %get-tuple-element.17.refs_2_, ...), custom_call_target="tpu_custom_call" | custom-call | tf_op jit(solution)/shard_map/pallas_call | solution.py:590

commit v4 on v3

--- a/solution.py
+++ b/solution.py
@@ -241,7 +241,6 @@
             res[0, 2 * j:2 * j + 2, :, :, cols] = (
                 dot(hidden, wo[:, cols]).astype(BF).reshape(2, 4, CAP, 256)
             )
-        give_back(0, j)
         arrt[:, span] = arr[0, 2 * j:2 * j + 2].reshape(256, D).T
 
     def backward_a(j):
@@ -278,22 +277,22 @@
         rcopy(ball.at[a, 0], ball.at[a, 0], rs_s.at[0], rs_r.at[a, n], along_z(1)).wait_recv()
 
     def rs(a, i):
+        totals = [combine(a, r, half) for half, r in (RS_UNITS[0][i], RS_UNITS[1][i])]
         if i >= 2:
             rs_await(a, i - 2)
         for d in range(2):
-            half, r = RS_UNITS[d][i]
-            prior = (half, r + 1 if d == 0 else r - 1)
-            total = combine(a, r, half)
-            if prior in RS_UNITS[d]:
+            total = totals[d]
+            if i >= 2:
                 total = total + rs_recv[a, d, i - 2].astype(F32)
             rs_send[a, d, i] = total.astype(BF)
             go(rs_copy(a, d, i))
 
     def rs_end(a, out):
+        totals = [combine(a, 0, half) for half in range(2)]
         rs_await(a, 5)
         rs_await(a, 6)
         for half in range(2):
-            total = combine(a, 0, half)
+            total = totals[half]
             for d in range(2):
                 n = RS_UNITS[d].index((half, 1 if d == 0 else 7))
                 total = total + rs_recv[a, d, n].astype(F32)
@@ -361,19 +360,15 @@
         go(wy_copy(w))
 
     def wend(w, out):
-        for i in (1, 5):
-            wx_copy(w, i).wait_recv()
-        total = wx_own[w, 1] + wx_recv[w, 1].astype(F32) + wx_recv[w, 5].astype(F32)
         wy_copy(w).wait_recv()
-        out[...] = total + wy_recv[w].astype(F32)
+        wx_copy(w, 1).wait_recv()
+        total = wx_own[w, 1] + wx_recv[w, 1].astype(F32) + wy_recv[w].astype(F32)
+        wx_copy(w, 5).wait_recv()
+        out[...] = total + wx_recv[w, 5].astype(F32)
 
     def backward(j):
         backward_a(j)
         backward_b(j)
-
-    def forward(j):
-        forward_a(j)
-        forward_b(j)
 
     build(0)
     dispatch(0, 0)
@@ -384,16 +379,14 @@
     meta_relay(1)
     build(7)
     build(1)
-    dispatch(1, 0)
+    turn_weights(1)
     ag_relay(0, 1, 1)
     dispatch(0, 7)
     dispatch(0, 1)
-    turn_weights(1)
     ag_relay(0, 2, 0)
     meta_relay(2)
     build(6)
     build(2)
-    turn_weights(2)
     ag_relay(0, 2, 1)
     dispatch(0, 6)
     dispatch(0, 2)
@@ -404,46 +397,56 @@
     build(5)
     build(3)
     forward_b(0)
+    give_back(0, 0)
     ag_relay(0, 3, 1)
     dispatch(0, 5)
     dispatch(0, 3)
+    forward_a(1)
     meta_relay(4)
     build(4)
-    forward(1)
     ag_relay(0, 4, 0)
     dispatch(0, 4)
-    turn_weights(3)
+    forward_b(1)
+    give_back(0, 1)
     ag_relay(1, 1, 0)
-    forward(2)
+    forward_a(2)
+    forward_b(2)
+    give_back(0, 2)
     ag_relay(1, 1, 1)
+    forward_a(3)
+    forward_b(3)
+    give_back(0, 3)
+    dispatch(1, 0)
     dispatch(1, 7)
     dispatch(1, 1)
-    forward(3)
     ag_relay(1, 2, 0)
+    turn_weights(2)
     ag_relay(1, 2, 1)
     dispatch(1, 6)
     dispatch(1, 2)
-    backward(0)
+    turn_weights(3)
     ag_relay(1, 3, 0)
-    rs(0, 0)
-    rs(0, 1)
-    backward(1)
     ag_relay(1, 3, 1)
     dispatch(1, 5)
     dispatch(1, 3)
+    rs(0, 0)
+    rs(0, 1)
+    backward(0)
     ag_relay(1, 4, 0)
     dispatch(1, 4)
     give_back(1, 0)
+    backward(1)
     give_back(1, 1)
-    backward(2)
-    give_back(1, 2)
     rs(0, 2)
+    await_rows(1, 2)
     await_rows(1, 3)
     wgrad(1, 2)
     wsend(1, 0)
     wgrad(1, 3)
     wsend(1, 4)
     rs(0, 3)
+    backward(2)
+    give_back(1, 2)
     backward(3)
     give_back(1, 3)
     rs(0, 4)
@@ -452,18 +455,18 @@
     wgrad(0, 3)
     wsend(0, 4)
     wsend(1, 3)
+    wsend(0, 3)
     rs(0, 5)
     wgrad(1, 1)
     wchain(1, 0)
-    wsend(0, 3)
     rs(0, 6)
+    wgrad(0, 1)
     rs(1, 0)
     rs(1, 1)
-    wgrad(0, 1)
+    wgrad(1, 0)
     wchain(0, 0)
     wsend(1, 1)
     wsend(0, 1)
-    wgrad(1, 0)
     rs_end(0, mixed_v)
     out_copy("mixed", mixed_v, mixed_o, 0)
     wgrad(0, 0)
@@ -471,25 +474,25 @@
         gate_grad(r)
     rs(1, 2)
     wchain(1, 1)
-    wfar(1)
     for r in (5, 2):
         gate_grad(r)
     rs(1, 3)
-    wchain(0, 1)
+    wfar(1)
     for r in (6, 1):
         gate_grad(r)
     rs(1, 4)
-    wfar(0)
     for r in (7, 0):
         gate_grad(r)
+    wchain(0, 1)
+    wfar(0)
     rs(1, 5)
+    rs(1, 6)
     rcopy(gg_send.at[1:8], gg_recv.at[1:8], gg_s.at[0], gg_r.at[0], along_z(1)).wait_recv()
     gg = gg_recv[0, 0:4, :]
     for r in range(1, 8):
         gg = gg + gg_recv[r, 0:4, :]
     gg_v[...] = gg
     out_copy("gg", gg_v, gg_o, 2)
-    rs(1, 6)
     wend(1, gout_v)
     out_copy("gout", gout_v, gout_o, 4)
     rs_end(1, tgrad_v)

time: 112 us -> 105 us (0.938)
  Pallas kernels: 111 us -> 103 us
    pallas_call x1, Pallas kernels: 109 us -> 101 us  [body(): pl.pallas_call(kernel, out_shape=shapes, in_specs=[anyspec] * 2 + [vmem]...]
where the time goes in v4:
time: 105 us; the launch traced here: 104 us
  Pallas kernels  103 us (98%)
    pallas_call x1, Pallas kernels, body(): pl.pallas_call(kernel, out_shape=shapes, in_specs=[anyspec] * 2 + [vmem]...  101 us
    pallas_call x1, Pallas kernels, body(): pl.pallas_call(hand_on, out_shape=shapes, in_specs=[anyspec] * 5, out_spe...  2.26 us

profile of v4, /device:TPU:1, one launch (start us, length us, event | category | flops | bytes accessed | tf_op | source)
XLA Modules:
  0.0 104.2 jit_solution(7483645917970533787)
XLA Ops:
  0.6 101.1 %shard_map.101 = (bf16[128,1024]{1,0:T(8,128)(2,1)}, bf16[128,1024]{1,0:T(8,128)(2,1)}, f32[4,128]{1,0:T(4,128)}, f32[128,1024]{1,0:T(8,128)}, f32[128,1024]{1,0:T(8,128)}) custom-call(bf16[128,1024]{1,0:T(8,128)(2,1)} %tok.1, bf16[128,1024]{1,0:T(8,128)(2,1)} %grd.1, s32[4,128]{1,0:T(4,128)} %bitcast.7, f32[4,128]{1,0:T(4,128)} %bitcast.8, ...), custom_call_target="tpu_custom_call" | custom-call | flops 14000000000 | bytes 8000000 | tf_op jit(solution)/shard_map/pallas_call | solution.py:580
  101.8 2.3 %shard_map.102 = (bf16[128,1024]{1,0:T(8,128)(2,1)}, bf16[128,1024]{1,0:T(8,128)(2,1)}, f32[4,128]{1,0:T(4,128)}, f32[128,1024]{1,0:T(8,128)}, f32[128,1024]{1,0:T(8,128)}) custom-call(bf16[128,1024]{1,0:T(8,128)(2,1)} %get-tuple-element.15.refs_0_, bf16[128,1024]{1,0:T(8,128)(2,1)} %get-tuple-element.16.refs_1_, f32[4,128]{1,0:T(4,128)} %get-tuple-element.17.refs_2_, ...), custom_call_target="tpu_custom_call" | custom-call | tf_op jit(solution)/shard_map/pallas_call | solution.py:593

commit v5 on v4

--- a/solution.py
+++ b/solution.py
@@ -44,9 +44,9 @@
 
 
 def kernel(
-    tok, grd, ids, gates, win, wout,
+    tok, grd, ids_o, gates_o, win, wout,
     mixed_o, tgrad_o, gg_o, gin_o, gout_o,
-    ball, metall, sel, selt, gatet, gslot, wi, wo, wit, wot,
+    ids, gates, ball, metall, sel, selt, gatet, gslot, wi, wo, wit, wot,
     disp, arr, arrt, actt, slope, pre, res, ret,
     mixed_v, tgrad_v, gg_v, gin_v, gout_v, hid,
     rs_send, rs_recv, gg_send, gg_recv,
@@ -95,17 +95,19 @@
         local[name] = pltpu.make_async_copy(src, dst, loc_sem.at[i])
         local[name].start()
 
+
+    def out_copy(name, src, dst, i):
+        lcopy(name, src, dst, 5 + i)
+
+    barrier = pltpu.get_barrier_semaphore()
+    for p in partners:
+        pl.semaphore_signal(barrier, inc=1, device_id=p, device_id_type=MESH)
+    lcopy("ids", ids_o, ids, 2)
+    lcopy("gates", gates_o, gates, 10)
     lcopy("x", tok, ball.at[0, 0], 0)
     lcopy("wi", win.at[0], wi, 3)
     lcopy("wo", wout.at[0], wo, 4)
     lcopy("g", grd, ball.at[1, 0], 1)
-
-    def out_copy(name, src, dst, i):
-        lcopy(name, src, dst, 5 + i)
-
-    barrier = pltpu.get_barrier_semaphore()
-    for p in partners:
-        pl.semaphore_signal(barrier, inc=1, device_id=p, device_id_type=MESH)
     pl.semaphore_wait(barrier, len(partners))
 
     own = (tok, grd)
@@ -144,6 +146,8 @@
 
     ag_own(0)
 
+    local["ids"].wait()
+    local["gates"].wait()
     expert = lax.broadcasted_iota(jnp.int32, (32, T), 0)
     named = [jnp.where(ids[k:k + 1, :] == expert, 1.0, 0.0) for k in range(4)]
     earlier = jnp.where(
@@ -523,9 +527,10 @@
 
 def body(tokens, expert_ids, gate_probs, out_grad, w_in, w_out):
     anyspec = pl.BlockSpec(memory_space=pl.ANY)
-    vmem = pl.BlockSpec(memory_space=pltpu.VMEM)
     dma = pltpu.SemaphoreType.DMA
     scratch = [
+        pltpu.VMEM((4, T), jnp.int32),
+        pltpu.VMEM((4, T), F32),
         pltpu.VMEM((2, 8, T, D), BF),
         pltpu.VMEM((8, 8, T), F32),
         pltpu.VMEM((8, T, T), BF),
@@ -560,7 +565,7 @@
         pltpu.VMEM((2, 2, 128, D), F32),
         pltpu.VMEM((2, 128, D), BF),
         pltpu.VMEM((2, 128, D), BF),
-        dma((10,)),
+        dma((11,)),
         dma((1,)), dma((2, 4, 2)),
         dma((1,)), dma((2, 4)),
         dma((1,)), dma((2, 4)),
@@ -580,7 +585,7 @@
     results = pl.pallas_call(
         kernel,
         out_shape=shapes,
-        in_specs=[anyspec] * 2 + [vmem] * 2 + [anyspec] * 2,
+        in_specs=[anyspec] * 6,
         out_specs=(anyspec,) * 5,
         scratch_shapes=scratch,
         compiler_params=pltpu.CompilerParams(

time: 105 us -> 104 us (level)
  no operation moved by 1% of the time
where the time goes in v5:
time: 104 us
  Pallas kernels  103 us (99%)
    pallas_call x1, Pallas kernels, body(): pl.pallas_call(kernel, out_shape=shapes, in_specs=[anyspec] * 6, out_spec...  101 us
    pallas_call x1, Pallas kernels, body(): pl.pallas_call(hand_on, out_shape=shapes, in_specs=[anyspec] * 5, out_spe...  2.26 us

profile of v5, /device:TPU:1, one launch (start us, length us, event | category | flops | bytes accessed | tf_op | source)
XLA Modules:
  0.0 103.6 jit_solution(16949643636082398188)
XLA Ops:
  0.6 100.5 %shard_map.101 = (bf16[128,1024]{1,0:T(8,128)(2,1)}, bf16[128,1024]{1,0:T(8,128)(2,1)}, f32[4,128]{1,0:T(4,128)}, f32[128,1024]{1,0:T(8,128)}, f32[128,1024]{1,0:T(8,128)}) custom-call(bf16[128,1024]{1,0:T(8,128)(2,1)} %tok.1, bf16[128,1024]{1,0:T(8,128)(2,1)} %grd.1, s32[4,128]{1,0:T(4,128)} %bitcast.7, f32[4,128]{1,0:T(4,128)} %bitcast.8, ...), custom_call_target="tpu_custom_call" | custom-call | flops 14000000000 | bytes 8000000 | tf_op jit(solution)/shard_map/pallas_call | solution.py:585
  101.2 2.3 %shard_map.102 = (bf16[128,1024]{1,0:T(8,128)(2,1)}, bf16[128,1024]{1,0:T(8,128)(2,1)}, f32[4,128]{1,0:T(4,128)}, f32[128,1024]{1,0:T(8,128)}, f32[128,1024]{1,0:T(8,128)}) custom-call(bf16[128,1024]{1,0:T(8,128)(2,1)} %get-tuple-element.15.refs_0_, bf16[128,1024]{1,0:T(8,128)(2,1)} %get-tuple-element.16.refs_1_, f32[4,128]{1,0:T(4,128)} %get-tuple-element.17.refs_2_, ...), custom_call_target="tpu_custom_call" | custom-call | tf_op jit(solution)/shard_map/pallas_call | solution.py:598

commit v6 on v5

--- a/solution.py
+++ b/solution.py
@@ -438,9 +438,7 @@
     backward(0)
     ag_relay(1, 4, 0)
     dispatch(1, 4)
-    give_back(1, 0)
     backward(1)
-    give_back(1, 1)
     rs(0, 2)
     await_rows(1, 2)
     await_rows(1, 3)
@@ -448,6 +446,8 @@
     wsend(1, 0)
     wgrad(1, 3)
     wsend(1, 4)
+    give_back(1, 0)
+    give_back(1, 1)
     rs(0, 3)
     backward(2)
     give_back(1, 2)

time: 104 us -> 103 us (level)
  no operation moved by 1% of the time
where the time goes in v6:
time: 103 us
  Pallas kernels  102 us (99%)
    pallas_call x1, Pallas kernels, body(): pl.pallas_call(kernel, out_shape=shapes, in_specs=[anyspec] * 6, out_spec...  100 us
    pallas_call x1, Pallas kernels, body(): pl.pallas_call(hand_on, out_shape=shapes, in_specs=[anyspec] * 5, out_spe...  2.26 us

profile of v6, /device:TPU:1, one launch (start us, length us, event | category | flops | bytes accessed | tf_op | source)
XLA Modules:
  0.0 103.2 jit_solution(2162015516867508640)
XLA Ops:
  0.6 100.1 %shard_map.101 = (bf16[128,1024]{1,0:T(8,128)(2,1)}, bf16[128,1024]{1,0:T(8,128)(2,1)}, f32[4,128]{1,0:T(4,128)}, f32[128,1024]{1,0:T(8,128)}, f32[128,1024]{1,0:T(8,128)}) custom-call(bf16[128,1024]{1,0:T(8,128)(2,1)} %tok.1, bf16[128,1024]{1,0:T(8,128)(2,1)} %grd.1, s32[4,128]{1,0:T(4,128)} %bitcast.7, f32[4,128]{1,0:T(4,128)} %bitcast.8, ...), custom_call_target="tpu_custom_call" | custom-call | flops 14000000000 | bytes 8000000 | tf_op jit(solution)/shard_map/pallas_call | solution.py:585
  100.7 2.3 %shard_map.102 = (bf16[128,1024]{1,0:T(8,128)(2,1)}, bf16[128,1024]{1,0:T(8,128)(2,1)}, f32[4,128]{1,0:T(4,128)}, f32[128,1024]{1,0:T(8,128)}, f32[128,1024]{1,0:T(8,128)}) custom-call(bf16[128,1024]{1,0:T(8,128)(2,1)} %get-tuple-element.15.refs_0_, bf16[128,1024]{1,0:T(8,128)(2,1)} %get-tuple-element.16.refs_1_, f32[4,128]{1,0:T(4,128)} %get-tuple-element.17.refs_2_, ...), custom_call_target="tpu_custom_call" | custom-call | tf_op jit(solution)/shard_map/pallas_call | solution.py:598
